TPU v7x, 256 devices: a whole 4x4x8 slice. The times are simulated.
256 devices in a mesh: dp: 2 (over core), mp: 128 (over z, y, x).
Axes of the slice: x: 4, y: 4, z: 8, core: 2. Of those that a mesh axis runs over, the one named last changes fastest.
Arguments:
- grad_parts: bfloat16 [2, 1536, 65536], P('dp', None, 'mp'), may hold values from -8000 to 8000
- owner: int32 [128, 3], P('mp'), may hold values from 0 to 1, as said below
- row_block: int32 [128, 3], P('mp'), may hold values from 0 to 2, as said below
- left_stats: float32 [128, 4, 512, 512], P('mp', 'dp'), may hold values from -1 to 6
- right_stats: float32 [128, 4, 512, 512], P('mp', 'dp'), may hold values from -1 to 6
- left_root: bfloat16 [128, 4, 512, 512], P('mp', 'dp'), may hold values from -1 to 6
- right_root: bfloat16 [128, 4, 512, 512], P('mp', 'dp'), may hold values from -1 to 6
- row_moment: float32 [128, 4, 512], P('mp', 'dp'), may hold values from 0.3 to 3
- col_moment: float32 [128, 4, 512], P('mp', 'dp'), may hold values from 0.3 to 3
Outputs:
- direction: bfloat16 [1536, 65536], P('dp', 'mp')
- new_left: float32 [128, 4, 512, 512], P('mp', 'dp')
- new_right: float32 [128, 4, 512, 512], P('mp', 'dp')
- new_rows: float32 [128, 4, 512], P('mp', 'dp')
- new_cols: float32 [128, 4, 512], P('mp', 'dp')
Inputs may be any that keep to these rules, and one draw needn't show every extreme that they name: In each column shard's list, every owner is named by at most 2 entries, and one owner by exactly 2. `row_block`: each column shard's list names every row block exactly once.
All inputs are finite; a program needn't handle non-finite values.
Results may differ from a plain program's by a relative error of at most 0.0058.
Values may be sent and summed in bfloat16 or wider, within the bound.
No kernel may reach another device: no remote copies, remote signals or barrier semaphores. Data moves between devices by JAX's collectives and lax.ppermute only.
A program may use at most 64 MiB of HBM per device.

v0:
```python
import jax
import jax.numpy as jnp
from jax import lax
from jax.sharding import PartitionSpec as P

DECAY_RATE = 0.95
PRECISE = lax.Precision.HIGHEST


def slot_numbers(owner_row, capacity):
    entry_count = owner_row.shape[0]
    positions = jnp.arange(entry_count, dtype=jnp.int32)
    earlier = positions[None, :] < positions[:, None]
    same_owner = owner_row[None, :] == owner_row[:, None]
    before = jnp.sum(jnp.where(earlier & same_owner, 1, 0).astype(jnp.int32), axis=1)
    return owner_row * capacity + before


def on_device(
    grad_parts,
    owner,
    row_block,
    left_stats,
    right_stats,
    left_root,
    right_root,
    row_moment,
    col_moment,
):
    local_part = grad_parts[0]
    rows_all, block_size = local_part.shape
    capacity = left_stats.shape[1]
    groups = lax.axis_size("dp")
    shard_rows = rows_all // groups
    entries_all = rows_all * block_size * lax.axis_size("mp")
    position = lax.axis_index("dp")
    slot_ids = slot_numbers(owner[0], capacity)
    blocks_row = row_block[0]
    block_count = blocks_row.shape[0]
    targets = position * capacity + jnp.arange(capacity, dtype=jnp.int32)
    matches = (slot_ids[None, :] == targets[:, None]).astype(jnp.int32)
    filled_count = jnp.sum(matches, axis=1)
    slot_total = groups * capacity
    onehot_slot = (slot_ids[:, None] == jnp.arange(slot_total, dtype=jnp.int32)[None, :]).astype(
        jnp.bfloat16
    )
    onehot_row = (blocks_row[:, None] == jnp.arange(block_count, dtype=jnp.int32)[None, :]).astype(
        jnp.bfloat16
    )
    selector = jnp.dot(onehot_slot.T, onehot_row, preferred_element_type=jnp.float32).astype(
        jnp.bfloat16
    )
    packed = jnp.dot(
        selector,
        local_part.reshape(block_count, block_size * block_size),
        preferred_element_type=jnp.float32,
    )
    packed = packed.reshape(slot_total, block_size, block_size)
    summed_blocks = lax.psum_scatter(packed, "dp", scatter_dimension=0, tiled=True)
    total_sq = lax.psum(jnp.sum(summed_blocks * summed_blocks), ("dp", "mp"))
    clip_factor = 1.0 / jnp.sqrt(total_sq / entries_all + 1e-06)
    blocks = summed_blocks * clip_factor
    gram_left = jnp.einsum("sij,skj->sik", blocks, blocks, precision=PRECISE)
    gram_right = jnp.einsum("sji,sjk->sik", blocks, blocks, precision=PRECISE)
    squares = blocks * blocks
    filled = filled_count[:, None, None] > 0
    kept_rows = filled_count[:, None] > 0
    stat_mix = (1.0 - DECAY_RATE) / block_size
    old_left = left_stats[0]
    old_right = right_stats[0]
    new_left = jnp.where(filled, DECAY_RATE * old_left + stat_mix * gram_left, old_left)
    new_right = jnp.where(filled, DECAY_RATE * old_right + stat_mix * gram_right, old_right)
    old_rows = row_moment[0]
    old_cols = col_moment[0]
    new_rows = jnp.where(
        kept_rows, DECAY_RATE * old_rows + (1.0 - DECAY_RATE) * jnp.mean(squares, axis=2), old_rows
    )
    new_cols = jnp.where(
        kept_rows, DECAY_RATE * old_cols + (1.0 - DECAY_RATE) * jnp.mean(squares, axis=1), old_cols
    )
    second = new_rows[:, :, None] * new_cols[:, None, :] / jnp.mean(new_rows, axis=1)[:, None, None]
    adam_step = blocks / (jnp.sqrt(second) + 1e-08)
    rounded = blocks.astype(jnp.bfloat16)
    half_done = jnp.einsum(
        "sik,skj->sij", left_root[0], rounded, preferred_element_type=jnp.float32
    ).astype(jnp.bfloat16)
    precond = jnp.einsum(
        "sik,skj->sij", half_done, right_root[0], preferred_element_type=jnp.float32
    )
    graft_ratio = jnp.sqrt(jnp.mean(adam_step * adam_step, axis=(1, 2))) / jnp.sqrt(
        jnp.mean(precond * precond, axis=(1, 2)) + 1e-06
    )
    update = (-graft_ratio[:, None, None] * precond).astype(jnp.bfloat16)
    every_update = lax.all_gather(update, "dp", axis=0, tiled=True)
    block_ids = jnp.arange(block_count, dtype=jnp.int32)
    slot_of_row = jnp.sum(
        jnp.where(blocks_row[None, :] == block_ids[:, None], slot_ids[None, :], 0), axis=1
    )
    pieces = []
    for which_block in range(block_count):
        chosen = lax.dynamic_index_in_dim(slot_of_row, which_block, 0, keepdims=False)
        pieces.append(lax.dynamic_index_in_dim(every_update, chosen, 0, keepdims=False))
    whole_column = jnp.concatenate(pieces, axis=0)
    direction = lax.dynamic_slice_in_dim(whole_column, position * shard_rows, shard_rows, 0)
    return (direction, new_left[None], new_right[None], new_rows[None], new_cols[None])


def solution(mesh):
    return jax.shard_map(
        on_device,
        mesh=mesh,
        in_specs=(
            P("dp", None, "mp"),
            P("mp", None),
            P("mp", None),
            P("mp", "dp", None, None),
            P("mp", "dp", None, None),
            P("mp", "dp", None, None),
            P("mp", "dp", None, None),
            P("mp", "dp", None),
            P("mp", "dp", None),
        ),
        out_specs=(
            P("dp", "mp"),
            P("mp", "dp", None, None),
            P("mp", "dp", None, None),
            P("mp", "dp", None),
            P("mp", "dp", None),
        ),
        check_vma=False,
    )
```

profile of v0, /device:TPU:1, one launch (start us, length us, event | category | flops | bytes accessed | tf_op | source)
XLA Modules:
  0.0 160.6 jit_solution(13944621535933697618)
XLA Ops:
  7.2 0.0 copy-start
  7.2 0.0 copy-start.6
  7.2 0.0 reduce-scatter.2.cloned.1.call-start
  7.2 0.9 select_reduce_fusion.1
  8.2 0.7 multiply_add_fusion
  8.8 2.5 %reshape_squeeze.3 = bf16[3,262144]{1,0:T(4,128)(2,1)S(1)} reshape(bf16[1,1536,512]{2,1,0:T(8,128)(2,1)} %param.9) | data formatting | bytes 3145728 | tf_op jit(solution)/shard_map/reshape;squeeze | solution.py:55
  11.3 0.0 copy-done.6
  11.3 3.4 %fusion.17 = f32[4,512,512]{2,0,1:T(4,128)} fusion(bf16[512,512,3]{1,2,0:T(4,128)(2,1)S(1)} %bitcast.82, s32[3]{0:T(128)S(1)} %bitcast.83, s32[3]{0:T(128)S(1)} %multiply_add_fusion), kind=kOutput, calls=%fused_computation.31 | convolution fusion | flops 6291561 | bytes 5767192 | tf_op jit(solution)/shard_map/dot_general | solution.py:53
  14.7 5.5 %copy.73 = f32[4,512,512]{2,1,0:T(8,128)} copy(f32[4,512,512]{2,0,1:T(4,128)} %fusion.17) | data formatting | bytes 8388608 | tf_op jit(solution)/shard_map/dot_general | solution.py:53
  20.2 0.0 copy-start.7
  20.2 0.0 reduce-scatter.2.cloned.1.call-update
  20.2 0.0 all-gather.2.cloned.1.call-start
  20.3 0.6 copy-done.7
  20.9 0.2 fusion.23
  21.1 0.0 copy-start.4
  21.1 0.0 copy-start.5
  21.1 21.1 %reduce-scatter.2.cloned.1.call-done = f32[2,512,512]{2,1,0:T(8,128)} async-done(((f32[4,512,512]{2,1,0:T(8,128)}), f32[2,512,512]{2,1,0:T(8,128)}) %reduce-scatter.2.cloned.1.call-update) | async-done | bytes 2097168 | tf_op jit(solution)/shard_map/reduce_scatter | solution.py:59
  42.1 0.0 copy-start.1
  42.1 2.9 %multiply_reduce_fusion.2 = f32[]{:T(128)} fusion(f32[2,512,512]{2,1,0:T(8,128)} %reduce-scatter.2.cloned.1.call-done), kind=kLoop, calls=%fused_computation.11 | loop fusion | flops 1048575 | bytes 2097156 | tf_op jit(solution)/shard_map/reduce_sum | solution.py:60
  45.0 77.7 %psum.7 = f32[]{:T(128)} all-reduce(f32[]{:T(128)} %multiply_reduce_fusion.2), channel_id=1, replica_groups=mesh['dp'=2,'mp'=128] {'dp','mp'}, use_global_device_ids=true, to_apply=%region_3.4 | all-reduce | flops 1 | bytes 8 | tf_op jit(solution)/shard_map/psum | solution.py:60
  123.5 0.0 copy-done.1
  123.5 0.4 multiply_reduce_fusion.3
  123.8 0.0 copy-done.4
  123.8 0.0 copy-done.5
  123.8 0.2 fusion.29
  124.0 0.0 copy-done
  124.1 4.0 %multiply_reduce_fusion = (f32[2]{0:T(128)S(1)}, f32[2,512,512]{2,1,0:T(8,128)}) fusion(bf16[1,2,512,512]{3,2,1,0:T(8,128)(2,1)S(1)} %copy-done, f32[2,512,512]{2,1,0:T(8,128)S(1)} %copy-done.1, bf16[1,2,512,512]{3,2,1,0:T(8,128)(2,1)} %param.14, f32[]{:T(128)S(6)} %sqrt.16), kind=kOutput, calls=%fused_computation.9 | convolution fusion | flops 1076363264 | bytes 6291468 | tf_op jit(solution)/shard_map/sik,skj->sij/dot_general | solution.py:87
  128.0 0.0 copy-start.2
  128.0 1.3 multiply_reduce_fusion.1
  129.4 0.2 copy-done.2
  129.6 1.3 multiply_convert_fusion
  131.0 0.0 all-gather.2.cloned.1.call-update
  131.0 0.1 select_reduce_fusion
  131.1 0.6 fusion.30
  137.5 0.7 fusion.18
  138.2 0.0 copy-start.3
  138.2 6.4 %fusion.1 = f32[1,2,512,512]{3,2,1,0:T(8,128)} fusion(f32[1,2,512,512]{3,2,1,0:T(8,128)} %param.13, f32[2,512,512]{2,1,0:T(8,128)S(1)} %copy-done.1, f32[]{:T(128)S(6)} %sqrt.16, pred[2]{0:T(512)(128)(4,1)S(1)} %broadcast_compare_fusion), kind=kOutput, calls=%fused_computation.3 | convolution fusion | flops 3223846912 | bytes 6291462 | tf_op jit(solution)/shard_map/sji,sjk->sik/dot_general | solution.py:64
  144.6 0.0 copy-done.3
  144.6 5.1 %fusion.3 = f32[1,2,512,512]{3,2,1,0:T(8,128)} fusion(f32[1,2,512,512]{3,2,1,0:T(8,128)S(1)} %copy-done.3, f32[2,512,512]{2,1,0:T(8,128)S(1)} %copy-done.1, f32[]{:T(128)S(6)} %sqrt.16, pred[2]{0:T(512)(128)(4,1)S(1)} %broadcast_compare_fusion), kind=kOutput, calls=%fused_computation.7 | convolution fusion | flops 3223846912 | bytes 6291462 | tf_op jit(solution)/shard_map/sij,skj->sik/dot_general | solution.py:63
  149.7 0.0 all-gather.2.cloned.1.call-done
  149.7 1.5 dynamic-slice_bitcast_fusion
  151.2 2.6 %fusion.16 = bf16[768,512]{1,0:T(8,128)(2,1)} fusion(s32[]{:T(128)S(6)} %select_n.60, bf16[512,512]{1,0:T(8,128)(2,1)S(1)} %get-tuple-element.26, bf16[512,512]{1,0:T(8,128)(2,1)S(1)} %get-tuple-element.25, bf16[512,512]{1,0:T(8,128)(2,1)S(1)} %get-tuple-element.24), kind=kLoop, calls=%fused_computation.30 | loop fusion | flops 2359296 | bytes 2359300 | tf_op jit(solution)/shard_map/concatenate | solution.py:103
  (5 shorter events, 0.0 us)
Async XLA Ops:
  7.2 116.9 %copy-start = (bf16[1,2,512,512]{3,2,1,0:T(8,128)(2,1)S(1)}, bf16[1,2,512,512]{3,2,1,0:T(8,128)(2,1)}, u32[]{:S(2)}) copy-start(bf16[1,2,512,512]{3,2,1,0:T(8,128)(2,1)} %param.15) | copy-start | bytes 3145732
  7.2 4.1 %copy-start.6 = (s32[1,3]{1,0:T(1,128)S(1)}, s32[1,3]{1,0:T(1,128)}, u32[]{:S(2)}) copy-start(s32[1,3]{1,0:T(1,128)} %param.11) | copy-start | bytes 40
  7.2 34.9 %reduce-scatter.2.cloned.1.call-start = ((), (), s32[]{:S(2)}) async-start(), calls=%async_computation.1 | async-start | bytes 6291456 | tf_op jit(solution)/shard_map/reduce_scatter | solution.py:59
  20.2 0.7 copy-start.7
  20.2 129.5 %all-gather.2.cloned.1.call-start = ((), (), s32[]{:S(2)}) async-start(), calls=%async_computation.2 | async-start | bytes 3145728 | tf_op jit(solution)/shard_map/all_gather | solution.py:94
  21.1 102.8 %copy-start.4 = (f32[1,2,512]{2,1,0:T(2,128)S(1)}, f32[1,2,512]{2,1,0:T(2,128)}, u32[]{:S(2)}) copy-start(f32[1,2,512]{2,1,0:T(2,128)} %param.16) | copy-start | bytes 12292
  21.1 102.8 %copy-start.5 = (f32[1,2,512]{2,1,0:T(2,128)S(1)}, f32[1,2,512]{2,1,0:T(2,128)}, u32[]{:S(2)}) copy-start(f32[1,2,512]{2,1,0:T(2,128)} %param.17) | copy-start | bytes 12292
  42.1 81.3 %copy-start.1 = (f32[2,512,512]{2,1,0:T(8,128)S(1)}, f32[2,512,512]{2,1,0:T(8,128)}, u32[]{:S(2)}) copy-start(f32[2,512,512]{2,1,0:T(8,128)} %reduce-scatter.2.cloned.1.call-done) | copy-start | bytes 6291460
  128.0 1.6 copy-start.2
  138.2 6.4 %copy-start.3 = (f32[1,2,512,512]{3,2,1,0:T(8,128)S(1)}, f32[1,2,512,512]{3,2,1,0:T(8,128)}, u32[]{:S(2)}) copy-start(f32[1,2,512,512]{3,2,1,0:T(8,128)} %param.12) | copy-start | bytes 6291460
Sparse Core Ops, SparseCore 0:
  20.4 21.7 reduce-scatter.1
  131.1 12.9 all-gather.1
where the time goes:
time: 161 us
  blocking collectives  77.7 us (48%)
  waiting for transfers between devices  21.1 us (13%)
  between operations  20.7 us (13%)
  matrix products  18.9 us (12%)
  other arithmetic  11.3 us (7%)
  local copies, waits for them, and re-layouts  10.8 us (7%)
    psum x1, blocking collectives, on_device(): total_sq = lax.psum(jnp.sum(summed_blocks * summed_blocks), ('dp', 'mp'))  77.7 us
    reduce_scatter x1, waiting for transfers between devices, on_device(): lax.psum_scatter(packed, 'dp', scatter_dimension=0, tiled=True)  21.1 us
    dot_general x1, matrix products, on_device(): gram_right = jnp.einsum('sji,sjk->sik', blocks, blocks, precision=PRECISE)  6.37 us
    dot_general x1, local copies, waits for them, and re-layouts, on_device(): jnp.dot(selector, local_part.reshape(block_count, block_size * block_size...  5.46 us
    dot_general x1, matrix products, on_device(): gram_left = jnp.einsum('sij,skj->sik', blocks, blocks, precision=PRECISE)  5.13 us
    dot_general x1, matrix products, on_device(): jnp.einsum('sik,skj->sij', half_done, right_root[0], preferred_element_ty...  3.99 us
    dot_general x1, matrix products, on_device(): jnp.dot(selector, local_part.reshape(block_count, block_size * block_size...  3.45 us
  transfers between devices with their start and end apart: 2, of which 1 were waited for; matrix products, arithmetic and copies ran while one was open for 8% of the time, Pallas kernels for 0%

commit v1 on v0

v1 whole, which is shorter than its diff:
```python
import functools

import jax
import jax.numpy as jnp
from jax import lax
from jax.experimental import pallas as pl
from jax.experimental.pallas import tpu as pltpu
from jax.sharding import PartitionSpec as P

DECAY = 0.95
SCALE = 1024.0
B = 512
BLK = 3
CAP = 2
HALF = B // 2
F32 = jnp.float32
BF16 = jnp.bfloat16
SWAP = [(0, 1), (1, 0)]
MIB = 1 << 20
VM = pl.BlockSpec(memory_space=pltpu.VMEM)
SM = pl.BlockSpec(memory_space=pltpu.SMEM)
HB = pl.BlockSpec(memory_space=pltpu.HBM)


def lanes_sum(x):
    return x[:, 0:128] + x[:, 128:256] + x[:, 256:384] + x[:, 384:512]


def scaled_sum(a, b):
    return (a.astype(F32) + b.astype(F32)) * SCALE


def square_kernel(g_ref, o_ref, out_ref):
    step = 64

    def body(i, acc):
        rows = pl.ds(pl.multiple_of(i * step, step), step)
        s = scaled_sum(g_ref[rows, :], o_ref[rows, :])
        s = s * s
        return acc + jnp.sum(s.reshape(step // 8, 8, B), axis=0)

    acc = lax.fori_loop(0, BLK * B // step, body, jnp.zeros((8, B), F32), unroll=4)
    out_ref[...] = jnp.sum(lanes_sum(acc), axis=0, keepdims=True)


def square_sum(g, o):
    return pl.pallas_call(
        square_kernel,
        out_shape=pltpu.VMEM((1, 128), F32),
        in_specs=[VM, VM],
        out_specs=VM,
        compiler_params=pltpu.CompilerParams(vmem_limit_bytes=8 * MIB),
        cost_estimate=pl.CostEstimate(
            flops=4 * BLK * B * B, bytes_accessed=4 * BLK * B * B, transcendentals=0
        ),
        name="squares",
    )(g, o)


def load_kernel(g_hbm, lroot_hbm, rroot_hbm, left_hbm, right_hbm, rows_hbm, cols_hbm,
                g_ref, lroot_ref, rroot_ref, left_ref, right_ref, moment_ref, rows_ref, cols_ref, sems):
    pairs = (
        (rows_hbm, rows_ref), (cols_hbm, cols_ref), (g_hbm, g_ref), (lroot_hbm, lroot_ref), (rroot_hbm, rroot_ref),
        (left_hbm, left_ref), (right_hbm, right_ref),
    )
    copies = [pltpu.make_async_copy(a, b, sems.at[i]) for i, (a, b) in enumerate(pairs)]
    for c in copies:
        c.start()
    for c in copies:
        c.wait()
    moment_ref[0:2, :] = rows_ref[...]
    moment_ref[2:4, :] = cols_ref[...]


def load(g, lroot, rroot, left, right, rows, cols):
    return pl.pallas_call(
        load_kernel,
        out_shape=(
            pltpu.VMEM((BLK * B, B), BF16),
            pltpu.VMEM((CAP, B, B), BF16),
            pltpu.VMEM((CAP, B, B), BF16),
            pltpu.VMEM((CAP, B, B), F32),
            pltpu.VMEM((CAP, B, B), F32),
            pltpu.VMEM((4, B), F32),
        ),
        in_specs=[HB] * 7,
        out_specs=(VM,) * 6,
        scratch_shapes=[
            pltpu.VMEM((CAP, B), F32),
            pltpu.VMEM((CAP, B), F32),
            pltpu.SemaphoreType.DMA((7,)),
        ],
        compiler_params=pltpu.CompilerParams(vmem_limit_bytes=2 * MIB),
        cost_estimate=pl.CostEstimate(flops=0, bytes_accessed=8 * MIB, transcendentals=0),
        name="load",
    )(*[pltpu.with_memory_space_constraint(a, pltpu.HBM) for a in (g, lroot, rroot, left, right, rows, cols)])


def slot_of_entry(owner_ref):
    o0, o1, o2 = owner_ref[0, 0], owner_ref[0, 1], owner_ref[0, 2]
    one = jnp.int32(1)
    zero = jnp.int32(0)
    s1 = jnp.where(o1 == o0, one, zero)
    s2 = jnp.where(o2 == o0, one, zero) + jnp.where(o2 == o1, one, zero)
    return (o0, o1, o2), (zero, s1, s2)


def rows_of_slots(owner_ref, row_ref, me):
    owners, slots = slot_of_entry(owner_ref)
    found = []
    for s in range(CAP):
        row, filled = jnp.int32(0), jnp.int32(0)
        for k in range(BLK):
            hit = (owners[k] == me) & (slots[k] == s)
            row = jnp.where(hit, row_ref[0, k], row)
            filled = jnp.where(hit, jnp.int32(1), filled)
        found.append((row, filled))
    return found


def entry_of_blocks(owner_ref, row_ref, me):
    owners, slots = slot_of_entry(owner_ref)
    found = []
    for b in range(BLK):
        mine, slot = jnp.int32(0), jnp.int32(0)
        for k in range(BLK):
            hit = row_ref[0, k] == b
            mine = jnp.where(hit & (owners[k] == me), jnp.int32(1), mine)
            slot = jnp.where(hit, slots[k], slot)
        found.append((mine, slot))
    return found


def product_kernel(owner_ref, row_ref, g_ref, o_ref, lroot_ref, rroot_ref, _, mine_ref, send_ref, psq_ref, tick_ref):
    me = lax.axis_index("dp")
    tick_ref[...] = jnp.zeros((1, 128), F32)
    pieces = []
    for s, (row, filled) in enumerate(rows_of_slots(owner_ref, row_ref, me)):
        rows = pl.ds(pl.multiple_of(row * B, B), B)
        block = scaled_sum(g_ref[rows, :], o_ref[rows, :]).astype(BF16)
        half = jnp.dot(lroot_ref[s], block, preferred_element_type=F32).astype(BF16)
        prod = jnp.dot(half, rroot_ref[s], preferred_element_type=F32)
        square = jnp.sum(lanes_sum(prod * prod), axis=0, keepdims=True)
        psq_ref[s : s + 1, :] = square
        for _ in range(3):
            piece = square.astype(BF16)
            square = square - piece.astype(F32)
            pieces.append(piece.astype(F32))
        prod = prod.astype(BF16)
        for h in range(2):
            chunk = 2 * row + h
            home = jnp.where(chunk >= 3, jnp.int32(1), jnp.int32(0))
            place = pl.ds(pl.multiple_of((chunk - 3 * home) * HALF, HALF), HALF)
            piece = prod[h * HALF : (h + 1) * HALF]

            @pl.when((filled == 1) & (home == me))
            def _():
                mine_ref[place, :] = piece

            @pl.when((filled == 1) & (home != me))
            def _():
                send_ref[place, :] = piece
    tail = jnp.concatenate(pieces + [jnp.zeros((10, 128), F32)], axis=0).astype(BF16)
    send_ref[BLK * HALF :, :] = jnp.concatenate([tail] * 4, axis=1)


def products(owner, row_block, g, o, lroot, rroot, after):
    return pl.pallas_call(
        product_kernel,
        out_shape=(
            pltpu.VMEM((BLK * HALF, B), BF16),
            pltpu.VMEM((BLK * HALF + 16, B), BF16),
            pltpu.VMEM((CAP, 128), F32),
            pltpu.VMEM((1, 128), F32),
        ),
        in_specs=[SM, SM] + [VM] * 5,
        out_specs=(VM,) * 4,
        compiler_params=pltpu.CompilerParams(vmem_limit_bytes=12 * MIB),
        cost_estimate=pl.CostEstimate(
            flops=100 * B * B * B, bytes_accessed=8 * MIB, transcendentals=0
        ),
        name="products",
    )(owner, row_block, g, o, lroot, rroot, after)


NT = (((1,), (1,)), ((), ()))
TN = (((0,), (0,)), ((), ()))


def gram(x, y, dims):
    return lax.dot_general(x, y, dims, preferred_element_type=F32)


def gram_kernel(
    owner_ref, row_ref, g_ref, o_ref, moment_ref, other_ref, _,
    gl_ref, gr_ref, sq_ref, rs_ref, rold_ref, vec_ref, flag_ref, tick_ref, cross_ref,
):
    me = lax.axis_index("dp")
    tick_ref[...] = jnp.zeros((1, 128), F32)
    for b, (mine, slot) in enumerate(entry_of_blocks(owner_ref, row_ref, me)):
        rows = slice(b * B, (b + 1) * B)
        s = scaled_sum(g_ref[rows, :], o_ref[rows, :])
        s = s * s
        sq_ref[b] = s
        rs_ref[b] = jnp.broadcast_to(jnp.sum(lanes_sum(s), axis=1, keepdims=True), (B, 128))
        vec_ref[4 + b : 5 + b, :] = jnp.sum(s, axis=0, keepdims=True)
        own = mine == 1
        first = slot == 0
        rold = jnp.where(
            own,
            jnp.where(first, moment_ref[0:1, :], moment_ref[1:2, :]),
            jnp.where(first, other_ref[0:1, :], other_ref[1:2, :]),
        )
        rold_ref[b] = jnp.broadcast_to(rold, (128, B)).T
        vec_ref[8 + b : 9 + b, :] = jnp.where(
            own,
            jnp.where(first, moment_ref[2:3, :], moment_ref[3:4, :]),
            jnp.where(first, other_ref[2:3, :], other_ref[3:4, :]),
        )
        flag_ref[b : b + 1, :] = jnp.full((1, 128), mine, jnp.int32).astype(F32)
        flag_ref[4 + b : 5 + b, :] = jnp.full((1, 128), slot, jnp.int32).astype(F32)
    for s, (row, filled) in enumerate(rows_of_slots(owner_ref, row_ref, me)):
        flag_ref[8 + s : 9 + s, :] = jnp.full((1, 128), filled, jnp.int32).astype(F32)
        vec_ref[s : s + 1, :] = rs_ref[row].T[0:1, :]
        vec_ref[2 + s : 3 + s, :] = vec_ref[pl.ds(4 + row, 1), :]
        rows = pl.ds(pl.multiple_of(row * B, B), B)
        block = scaled_sum(g_ref[rows, :], o_ref[rows, :])
        hi = block.astype(BF16)
        lo = (block - hi.astype(F32)).astype(BF16)
        for out, dims in ((gl_ref, NT), (gr_ref, TN)):
            cross_ref[...] = gram(hi, lo, dims)
            out[s] = gram(hi, hi, dims)
            out[s] = out[s] + cross_ref[...] + cross_ref[...].T


def grams(owner, row_block, g, o, moments, others, after):
    return pl.pallas_call(
        gram_kernel,
        out_shape=(
            pltpu.VMEM((CAP, B, B), F32),
            pltpu.VMEM((CAP, B, B), F32),
            pltpu.VMEM((BLK, B, B), F32),
            pltpu.VMEM((BLK, B, 128), F32),
            pltpu.VMEM((BLK, B, 128), F32),
            pltpu.VMEM((16, B), F32),
            pltpu.VMEM((16, 128), F32),
            pltpu.VMEM((1, 128), F32),
        ),
        in_specs=[SM, SM] + [VM] * 5,
        out_specs=(VM,) * 8,
        scratch_shapes=[pltpu.VMEM((B, B), F32)],
        compiler_params=pltpu.CompilerParams(vmem_limit_bytes=12 * MIB),
        cost_estimate=pl.CostEstimate(
            flops=400 * B * B * B, bytes_accessed=12 * MIB, transcendentals=0
        ),
        name="grams",
    )(owner, row_block, g, o, moments, others, after)


def finish_kernel(
    total_ref, gl_ref, gr_ref, sq_ref, rs_ref, rold_ref, vec_ref, flag_ref,
    left_ref, right_ref, moment_ref, mine_ref, recv_ref, psq_ref,
    dir_hbm, nl_hbm, nr_hbm, nrows_hbm, ncols_hbm,
    nl_ref, nr_ref, dir_ref, nrows_ref, ncols_ref, sems, *, entries
):
    me = lax.axis_index("dp")
    total = jnp.sum(total_ref[...].reshape(-1, 128), axis=0, keepdims=True)
    total = jnp.sum(total, axis=1, keepdims=True)
    clip = lax.rsqrt(total * (1.0 / (SCALE * SCALE * entries)) + 1e-6) * (1.0 / SCALE)
    clip2 = clip * clip
    mix = (1.0 - DECAY) / B * clip2
    copies = []

    def send_out(src, dst, sem):
        copies.append(pltpu.make_async_copy(src, dst, sems.at[sem]))
        copies[-1].start()

    for s in range(CAP):
        filled = flag_ref[8 + s : 9 + s, 0:1]
        keep = 1.0 - (1.0 - DECAY) * filled
        add = mix * filled
        nrows_ref[s : s + 1, :] = keep * moment_ref[s : s + 1, :] + add * vec_ref[s : s + 1, :]
        ncols_ref[s : s + 1, :] = keep * moment_ref[2 + s : 3 + s, :] + add * vec_ref[2 + s : 3 + s, :]
        nl_ref[s] = keep * left_ref[s] + add * gl_ref[s]
        send_out(nl_ref.at[s], nl_hbm.at[s], 2 * s)
        nr_ref[s] = keep * right_ref[s] + add * gr_ref[s]
        send_out(nr_ref.at[s], nr_hbm.at[s], 2 * s + 1)
    send_out(nrows_ref, nrows_hbm, 4)
    send_out(ncols_ref, ncols_hbm, 5)
    factors, owns = [], []
    for i in range(2):
        b = me + i
        new_rows = DECAY * rold_ref[b] + mix * rs_ref[b]
        mean = jnp.sum(new_rows, axis=0, keepdims=True) * (1.0 / B)
        u = jnp.sqrt(new_rows / mean)
        v = jnp.sqrt(DECAY * vec_ref[pl.ds(8 + b, 1), :] + mix * vec_ref[pl.ds(4 + b, 1), :])
        acc = jnp.zeros((8, 128), F32)
        for j in range(4):
            cols = slice(128 * j, 128 * (j + 1))
            r = 1.0 / (u * v[:, cols] + 1e-8)
            acc = acc + jnp.sum((sq_ref[b, :, cols] * r * r).reshape(B // 8, 8, 128), axis=0)
        adam = jnp.sum(jnp.sum(acc, axis=0, keepdims=True), axis=1, keepdims=True)
        adam = adam * clip2 * (1.0 / (B * B))
        own = flag_ref[pl.ds(b, 1), :] > 0.5
        first = flag_ref[pl.ds(4 + b, 1), :] < 0.5
        tail = recv_ref[BLK * HALF :, 0:128].astype(F32)
        psq = jnp.where(
            own,
            jnp.where(first, psq_ref[0:1, :], psq_ref[1:2, :]),
            jnp.where(
                first,
                tail[0:1] + tail[1:2] + tail[2:3],
                tail[3:4] + tail[4:5] + tail[5:6],
            ),
        )
        psq = jnp.sum(psq, axis=1, keepdims=True) * clip2 * (1.0 / (B * B))
        factors.append(-clip * jnp.sqrt(adam) * lax.rsqrt(psq + 1e-6))
        owns.append(flag_ref[pl.ds(b, 1), 0:1])
    at_one = me == 1
    for j in range(BLK):
        rows = slice(j * HALF, (j + 1) * HALF)
        low, high = j // 2, (j + 1) // 2
        factor = jnp.where(at_one, factors[high], factors[low])
        own = jnp.where(at_one, owns[high], owns[low])
        piece = jnp.where(own > 0.5, mine_ref[rows, :].astype(F32), recv_ref[rows, :].astype(F32))
        dir_ref[rows, :] = (piece * factor).astype(BF16)
        send_out(dir_ref.at[rows, :], dir_hbm.at[rows, :], 6 + j)
    for c in copies:
        c.wait()


def finish(entries, *args):
    return pl.pallas_call(
        functools.partial(finish_kernel, entries=entries),
        out_shape=(
            jax.ShapeDtypeStruct((BLK * HALF, B), BF16),
            jax.ShapeDtypeStruct((CAP, B, B), F32),
            jax.ShapeDtypeStruct((CAP, B, B), F32),
            jax.ShapeDtypeStruct((CAP, B), F32),
            jax.ShapeDtypeStruct((CAP, B), F32),
        ),
        in_specs=[VM] * 14,
        out_specs=(HB,) * 5,
        scratch_shapes=[
            pltpu.VMEM((CAP, B, B), F32),
            pltpu.VMEM((CAP, B, B), F32),
            pltpu.VMEM((BLK * HALF, B), BF16),
            pltpu.VMEM((CAP, B), F32),
            pltpu.VMEM((CAP, B), F32),
            pltpu.SemaphoreType.DMA((9,)),
        ],
        compiler_params=pltpu.CompilerParams(vmem_limit_bytes=12 * MIB),
        cost_estimate=pl.CostEstimate(
            flops=16 * B * B, bytes_accessed=16 * MIB, transcendentals=0
        ),
        name="finish",
    )(*args)


def mp_swap(v, peer):
    pairs = []
    for z in range(8):
        for y in range(4):
            for x in range(4):
                to_z, to_y, to_x = peer(z, y, x)
                pairs.append(((z * 4 + y) * 4 + x, (to_z * 4 + to_y) * 4 + to_x))
    size = lax.axis_size("mp")
    return v + lax.ppermute(v, "mp", [p for p in pairs if max(p) < size])


def around(c, odd, size):
    return (((c + odd) ^ 1) - odd) % size


def swap_x(v, odd):
    return mp_swap(v, lambda z, y, x: (z, y, around(x, odd, 4)))


def rest_chips(v):
    if lax.axis_size("mp") != 128:
        return v
    groups = [[k * 4 + x for k in range(32)] for x in range(4)]
    many = jnp.broadcast_to(v, (32, 128))
    return lax.all_to_all(many, "mp", 0, 0, tiled=True, axis_index_groups=groups)


def on_device(
    grad_parts, owner, row_block, left_stats, right_stats, left_root, right_root, row_moment, col_moment
):
    entries = BLK * B * B * lax.axis_size("mp")
    o = lax.ppermute(grad_parts[0], "dp", SWAP)
    g, lroot, rroot, left, right, moments = load(
        grad_parts[0], left_root[0], right_root[0], left_stats[0], right_stats[0], row_moment[0], col_moment[0]
    )
    others = lax.ppermute(moments, "dp", SWAP)
    part = square_sum(g, o)
    mine, send, psq, tick = products(owner, row_block, g, o, lroot, rroot, part)
    recv = lax.ppermute(send, "dp", SWAP)
    part = swap_x(part, 0) + tick
    gl, gr, sq, rs, rold, vec, flag, tick = grams(owner, row_block, g, o, moments, others, part)
    total = rest_chips(swap_x(part, 1) + tick)
    direction, new_left, new_right, new_rows, new_cols = finish(
        entries, total, gl, gr, sq, rs, rold, vec, flag, left, right, moments, mine, recv, psq
    )
    return (direction, new_left[None], new_right[None], new_rows[None], new_cols[None])


def solution(mesh):
    return jax.shard_map(
        on_device,
        mesh=mesh,
        in_specs=(
            P("dp", None, "mp"),
            P("mp", None),
            P("mp", None),
            P("mp", "dp", None, None),
            P("mp", "dp", None, None),
            P("mp", "dp", None, None),
            P("mp", "dp", None, None),
            P("mp", "dp", None),
            P("mp", "dp", None),
        ),
        out_specs=(
            P("dp", "mp"),
            P("mp", "dp", None, None),
            P("mp", "dp", None, None),
            P("mp", "dp", None),
            P("mp", "dp", None),
        ),
        check_vma=False,
    )
```

time: 161 us -> 39.6 us (0.25)
  blocking collectives: 77.7 us -> 19.6 us
  waiting for transfers between devices: 21.1 us -> 0.01 us
  between operations: 20.7 us -> 0.73 us
  matrix products: 18.9 us -> 0 us
  Pallas kernels: 0 us -> 13.5 us
  other arithmetic: 11.3 us -> 0.01 us
  local copies, waits for them, and re-layouts: 10.8 us -> 0.02 us
  starting transfers between devices: 0.08 us -> 5.59 us
    psum x1 -> x0, blocking collectives: 77.7 us -> none  [on_device(): total_sq = lax.psum(jnp.sum(summed_blocks * summed_blocks), ('dp', 'mp'))]
    reduce_scatter x1 -> x0, waiting for transfers between devices: 21.1 us -> none  [on_device(): lax.psum_scatter(packed, 'dp', scatter_dimension=0, tiled=True)]
    all_to_all x0 -> x1, blocking collectives: none -> 19.6 us  [rest_chips(): lax.all_to_all(many, 'mp', 0, 0, tiled=True, axis_index_groups=groups)]
    dot_general x4 -> x0, matrix products: 18.9 us -> none  [the longest x1 6.37 us: on_device(): gram_right = jnp.einsum('sji,sjk->sik', blocks, blocks, precision=PRECISE)]
    pallas_call x0 -> x5, Pallas kernels: none -> 13.5 us  [the longest x1 3.82 us: grams(): pl.pallas_call(gram_kernel, out_shape=(pltpu.VMEM((CAP, B, B), F32), pltp...]
    reduce_sum x7 -> x0, other arithmetic: 6 us -> none  [the longest x1 2.88 us: on_device(): total_sq = lax.psum(jnp.sum(summed_blocks * summed_blocks), ('dp', 'mp'))]
    ppermute x0 -> x5, starting transfers between devices: none -> 5.59 us  [the longest x1 3.33 us: on_device(): o = lax.ppermute(grad_parts[0], 'dp', SWAP)]
    dot_general x1 -> x0, local copies, waits for them, and re-layouts: 5.46 us -> none  [on_device(): jnp.dot(selector, local_part.reshape(block_count, block_size * block_size...]
  transfers between devices with their start and end apart: 2 -> 5, of which waited for: 1 -> 0; matrix products, arithmetic and copies ran while one was open for 8% -> 0% of each run, Pallas kernels for 0% -> 26%
where the time goes in v1:
time: 39.6 us; the launch traced here: 39.5 us
  blocking collectives  19.6 us (49%)
  Pallas kernels  13.5 us (34%)
  starting transfers between devices  5.59 us (14%)
  between operations  0.73 us (2%)
    all_to_all x1, blocking collectives, rest_chips(): lax.all_to_all(many, 'mp', 0, 0, tiled=True, axis_index_groups=groups)  19.6 us
    pallas_call x1, Pallas kernels, grams(): pl.pallas_call(gram_kernel, out_shape=(pltpu.VMEM((CAP, B, B), F32), pltp...  3.82 us
    pallas_call x1, Pallas kernels, load(): pl.pallas_call(load_kernel, out_shape=(pltpu.VMEM((BLK * B, B), BF16), pl...  3.41 us
    ppermute x1, starting transfers between devices, on_device(): o = lax.ppermute(grad_parts[0], 'dp', SWAP)  3.33 us
    pallas_call x1, Pallas kernels, finish(): pl.pallas_call(functools.partial(finish_kernel, entries=entries), out_sha...  3.3 us
    pallas_call x1, Pallas kernels, products(): pl.pallas_call(product_kernel, out_shape=(pltpu.VMEM((BLK * HALF, B), BF1...  2.26 us
    ppermute x2, starting transfers between devices, mp_swap(): return v + lax.ppermute(v, 'mp', [p for p in pairs if max(p) < size])  1.64 us
  transfers between devices with their start and end apart: 5, of which 0 were waited for; matrix products, arithmetic and copies ran while one was open for 0% of the time, Pallas kernels for 26%

profile of v1, /device:TPU:1, one launch (start us, length us, event | category | flops | bytes accessed | tf_op | source)
XLA Modules:
  0.0 39.5 jit_solution(5524597687794277903)
XLA Ops:
  0.6 3.3 %collective-permute-start = (bf16[1536,512]{1,0:T(8,128)(2,1)}, bf16[1536,512]{1,0:T(8,128)(2,1)S(1)}, u32[]{:S(2)}, u32[]{:S(2)}) collective-permute-start(bf16[1536,512]{1,0:T(8,128)(2,1)} %bitcast.17), channel_id=1, source_target_pairs={{0,128},{128,0},{1,129},{129,1},{2,130},{130,2},{3,131},{131,3},{4... | collective-permute-start | bytes 4718600 | tf_op jit(solution)/shard_map/ppermute | solution.py:391
  4.0 3.4 %load.1 = (bf16[1536,512]{1,0:T(8,128)(2,1)S(1)}, bf16[2,512,512]{2,1,0:T(8,128)(2,1)S(1)}, bf16[2,512,512]{2,1,0:T(8,128)(2,1)S(1)}, f32[2,512,512]{2,1,0:T(8,1...) custom-call(bf16[1536,512]{1,0:T(8,128)(2,1)} %bitcast.18, bf16[2,512,512]{2,1,0:T(8,128)(2,1)} %bitcast.19, ...), custom_call_target="tpu_custom_call" | custom-call | bytes 8388608 | tf_op jit(solution)/shard_map/load/pallas_call | solution.py:76
  7.4 0.0 copy-start
  7.4 0.0 copy-start.1
  7.4 0.1 collective-permute-start.3
  7.5 0.0 collective-permute-done.o_ref
  7.5 0.7 %squares.1._ = f32[1,128]{1,0:T(1,128)S(1)} custom-call(bf16[1536,512]{1,0:T(8,128)(2,1)S(1)} %get-tuple-element.28.g_ref, bf16[1536,512]{1,0:T(8,128)(2,1)S(1)} %collective-permute-done.o_ref), custom_call_target="tpu_custom_call" | custom-call | flops 3145728 | bytes 3145728 | tf_op jit(solution)/shard_map/squares/pallas_call | solution.py:47
  8.2 0.1 collective-permute-start.1
  8.3 0.0 copy-done
  8.3 0.0 copy-done.1
  8.3 2.3 %products.1 = (bf16[768,512]{1,0:T(8,128)(2,1)S(1)}, bf16[784,512]{1,0:T(8,128)(2,1)S(1)}, f32[2,128]{1,0:T(2,128)S(1)}, f32[1,128]{1,0:T(1,128)S(1)}) custom-call(s32[1,3]{1,0:T(1,128)S(1)} %copy-done, s32[1,3]{1,0:T(1,128)S(1)} %copy-done.1, bf16[1536,512]{1,0:T(8,128)(2,1)S(1)} %get-tuple-element.28.g_ref, ...), custom_call_target="tpu_custom_call" | custom-call | flops 13421772800 | bytes 8388608 | tf_op jit(solution)/shard_map/products/pallas_call | solution.py:168
  10.6 0.5 %collective-permute-start.4 = (bf16[784,512]{1,0:T(8,128)(2,1)S(1)}, bf16[784,512]{1,0:T(8,128)(2,1)S(1)}, u32[]{:S(2)}, u32[]{:S(2)}) collective-permute-start(bf16[784,512]{1,0:T(8,128)(2,1)S(1)} %get-tuple-element.44), channel_id=1, source_target_pairs={{0,128},{128,0},{1,129},{129,1},{2,130},{130,2},{3,131},{131,3},{4... | collective-permute-start | bytes 2408456 | tf_op jit(solution)/shard_map/ppermute | solution.py:398
  11.1 0.0 collective-permute-done.1
  11.1 1.5 %collective-permute-start.2 = (f32[1,128]{1,0:T(1,128)S(1)}, f32[1,128]{1,0:T(1,128)S(1)}, u32[]{:S(2)}, u32[]{:S(2)}) collective-permute-start(f32[1,128]{1,0:T(1,128)S(1)} %add_add_fusion._), channel_id=1, source_target_pairs={{0,3},{1,2},{2,1},{3,0},{4,7},{5,6},{6,5},{7,4},{8,11},{9,10},{10,... | collective-permute-start | bytes 1544 | tf_op jit(solution)/shard_map/ppermute | solution.py:368
  12.6 0.0 collective-permute-done.3.other_ref
  12.7 3.8 %grams.1 = (f32[2,512,512]{2,1,0:T(8,128)S(1)}, f32[2,512,512]{2,1,0:T(8,128)S(1)}, f32[3,512,512]{2,1,0:T(8,128)S(1)}, f32[3,512,128]{2,1,0:T(8,128)S(1)}, f32[...) custom-call(s32[1,3]{1,0:T(1,128)S(1)} %copy-done, ...), custom_call_target="tpu_custom_call" | custom-call | flops 53687091200 | bytes 12582912 | tf_op jit(solution)/shard_map/grams/pallas_call | solution.py:237
  16.5 0.0 collective-permute-done.2
  16.5 19.6 %all_to_all.8 = f32[32,1,128]{2,1,0:T(1,128)S(1)} all-to-all(f32[32,1,128]{2,1,0:T(1,128)S(1)} %broadcast_in_dim.17), channel_id=1, replica_groups={{0,4,8,12,16,20,24,28,32,36,40,44,48,52,56,60,64,68,72,76,80,84,88,92,9..., dimensions={0} | all-to-all | bytes 32768 | tf_op jit(solution)/shard_map/all_to_all | solution.py:384
  36.2 0.0 collective-permute-done.4.recv_ref
  36.2 3.3 %finish.1 = (bf16[768,512]{1,0:T(8,128)(2,1)}, f32[2,512,512]{2,1,0:T(8,128)}, f32[2,512,512]{2,1,0:T(8,128)}, f32[2,512]{1,0:T(2,128)}, f32[2,512]{1,0:T(2,128)}) custom-call(f32[32,128]{1,0:T(8,128)S(1)} %bitcast.14, f32[2,512,512]{2,1,0:T(8,128)S(1)} %get-tuple-element.34.gl_ref, f32[2,512,512]{2,1,0:T(8,128)S(1)} %get-tuple-element.35.gr_ref, ...), custom_call_target="tpu_custom_call" | custom-call | flops 4194304 | bytes 16777216 | tf_op jit(solution)/shard_map/finish/pallas_call | solution.py:333
  (3 shorter events, 0.0 us)
Async XLA Ops:
  0.6 6.9 %collective-permute-start = (bf16[1536,512]{1,0:T(8,128)(2,1)}, bf16[1536,512]{1,0:T(8,128)(2,1)S(1)}, u32[]{:S(2)}, u32[]{:S(2)}) collective-permute-start(bf16[1536,512]{1,0:T(8,128)(2,1)} %bitcast.17), channel_id=1, source_target_pairs={{0,128},{128,0},{1,129},{129,1},{2,130},{130,2},{3,131},{131,3},{4... | collective-permute-start | bytes 4718600 | tf_op jit(solution)/shard_map/ppermute | solution.py:391
  7.4 0.9 %copy-start = (s32[1,3]{1,0:T(1,128)S(1)}, s32[1,3]{1,0:T(1,128)}, u32[]{:S(2)}) copy-start(s32[1,3]{1,0:T(1,128)} %owner_ref.3) | copy-start | bytes 40
  7.4 0.9 %copy-start.1 = (s32[1,3]{1,0:T(1,128)S(1)}, s32[1,3]{1,0:T(1,128)}, u32[]{:S(2)}) copy-start(s32[1,3]{1,0:T(1,128)} %row_ref.3) | copy-start | bytes 40
  7.4 5.2 %collective-permute-start.3 = (f32[4,512]{1,0:T(4,128)S(1)}, f32[4,512]{1,0:T(4,128)S(1)}, u32[]{:S(2)}, u32[]{:S(2)}) collective-permute-start(f32[4,512]{1,0:T(4,128)S(1)} %get-tuple-element.32.moment_ref), channel_id=1, source_target_pairs={{0,128},{128,0},{1,129},{129,1},{2,130},{130,2},{3,131},{131,3},{4... | collective-permute-start | bytes 24584 | tf_op jit(solution)/shard_map/ppermute | solution.py:395
  8.2 2.9 %collective-permute-start.1 = (f32[1,128]{1,0:T(1,128)S(1)}, f32[1,128]{1,0:T(1,128)S(1)}, u32[]{:S(2)}, u32[]{:S(2)}) collective-permute-start(f32[1,128]{1,0:T(1,128)S(1)} %squares.1._), channel_id=1, source_target_pairs={{0,1},{1,0},{2,3},{3,2},{4,5},{5,4},{6,7},{7,6},{8,9},{9,8},{10,11... | collective-permute-start | bytes 1544 | tf_op jit(solution)/shard_map/ppermute | solution.py:368
  10.6 25.6 %collective-permute-start.4 = (bf16[784,512]{1,0:T(8,128)(2,1)S(1)}, bf16[784,512]{1,0:T(8,128)(2,1)S(1)}, u32[]{:S(2)}, u32[]{:S(2)}) collective-permute-start(bf16[784,512]{1,0:T(8,128)(2,1)S(1)} %get-tuple-element.44), channel_id=1, source_target_pairs={{0,128},{128,0},{1,129},{129,1},{2,130},{130,2},{3,131},{131,3},{4... | collective-permute-start | bytes 2408456 | tf_op jit(solution)/shard_map/ppermute | solution.py:398
  11.1 5.4 %collective-permute-start.2 = (f32[1,128]{1,0:T(1,128)S(1)}, f32[1,128]{1,0:T(1,128)S(1)}, u32[]{:S(2)}, u32[]{:S(2)}) collective-permute-start(f32[1,128]{1,0:T(1,128)S(1)} %add_add_fusion._), channel_id=1, source_target_pairs={{0,3},{1,2},{2,1},{3,0},{4,7},{5,6},{6,5},{7,4},{8,11},{9,10},{10,... | collective-permute-start | bytes 1544 | tf_op jit(solution)/shard_map/ppermute | solution.py:368

commit v2 on v1

v2 whole, which is shorter than its diff:
```python
import functools

import jax
import jax.numpy as jnp
from jax import lax
from jax.experimental import pallas as pl
from jax.experimental.pallas import tpu as pltpu
from jax.sharding import PartitionSpec as P

DECAY = 0.95
SCALE = 1024.0
B = 512
BLK = 3
CAP = 2
HALF = B // 2
TAIL = 32
F32 = jnp.float32
BF16 = jnp.bfloat16
SWAP = [(0, 1), (1, 0)]
MIB = 1 << 20
VM = pl.BlockSpec(memory_space=pltpu.VMEM)
SM = pl.BlockSpec(memory_space=pltpu.SMEM)
HB = pl.BlockSpec(memory_space=pltpu.HBM)


def lanes_sum(x):
    return x[:, 0:128] + x[:, 128:256] + x[:, 256:384] + x[:, 384:512]


def scaled_sum(a, b):
    return (a.astype(F32) + b.astype(F32)) * SCALE


def square_kernel(g_ref, o_ref, out_ref):
    step = 64

    def body(i, acc):
        rows = pl.ds(pl.multiple_of(i * step, step), step)
        s = g_ref[rows, :].astype(F32) + o_ref[rows, :].astype(F32)
        s = s * s
        return acc + jnp.sum(s.reshape(step // 8, 8, B), axis=0)

    acc = lax.fori_loop(0, BLK * B // step, body, jnp.zeros((8, B), F32), unroll=4)
    out_ref[...] = jnp.sum(lanes_sum(acc), axis=0, keepdims=True)


def square_sum(g, o):
    return pl.pallas_call(
        square_kernel,
        out_shape=pltpu.VMEM((1, 128), F32),
        in_specs=[VM, VM],
        out_specs=VM,
        compiler_params=pltpu.CompilerParams(vmem_limit_bytes=8 * MIB),
        cost_estimate=pl.CostEstimate(
            flops=4 * BLK * B * B, bytes_accessed=4 * BLK * B * B, transcendentals=0
        ),
        name="squares",
    )(g, o)


def load_kernel(g_hbm, lroot_hbm, rroot_hbm, left_hbm, right_hbm, rows_hbm, cols_hbm,
                g_ref, lroot_ref, rroot_ref, left_ref, right_ref, moment_ref, rows_ref, cols_ref, sems):
    pairs = (
        (rows_hbm, rows_ref), (cols_hbm, cols_ref), (g_hbm, g_ref), (lroot_hbm, lroot_ref), (rroot_hbm, rroot_ref),
        (left_hbm, left_ref), (right_hbm, right_ref),
    )
    copies = [pltpu.make_async_copy(a, b, sems.at[i]) for i, (a, b) in enumerate(pairs)]
    for c in copies:
        c.start()
    for c in copies:
        c.wait()
    moment_ref[0:2, :] = rows_ref[...]
    moment_ref[2:4, :] = cols_ref[...]


def load(g, lroot, rroot, left, right, rows, cols):
    return pl.pallas_call(
        load_kernel,
        out_shape=(
            pltpu.VMEM((BLK * B, B), BF16),
            pltpu.VMEM((CAP, B, B), BF16),
            pltpu.VMEM((CAP, B, B), BF16),
            pltpu.VMEM((CAP, B, B), F32),
            pltpu.VMEM((CAP, B, B), F32),
            pltpu.VMEM((4, B), F32),
        ),
        in_specs=[HB] * 7,
        out_specs=(VM,) * 6,
        scratch_shapes=[
            pltpu.VMEM((CAP, B), F32),
            pltpu.VMEM((CAP, B), F32),
            pltpu.SemaphoreType.DMA((7,)),
        ],
        compiler_params=pltpu.CompilerParams(vmem_limit_bytes=2 * MIB),
        cost_estimate=pl.CostEstimate(flops=0, bytes_accessed=8 * MIB, transcendentals=0),
        name="load",
    )(*[pltpu.with_memory_space_constraint(a, pltpu.HBM) for a in (g, lroot, rroot, left, right, rows, cols)])


def slot_of_entry(owner_ref):
    o0, o1, o2 = owner_ref[0, 0], owner_ref[0, 1], owner_ref[0, 2]
    one = jnp.int32(1)
    zero = jnp.int32(0)
    s1 = jnp.where(o1 == o0, one, zero)
    s2 = jnp.where(o2 == o0, one, zero) + jnp.where(o2 == o1, one, zero)
    return (o0, o1, o2), (zero, s1, s2)


def rows_of_slots(owner_ref, row_ref, me):
    owners, slots = slot_of_entry(owner_ref)
    found = []
    for s in range(CAP):
        row, filled = jnp.int32(0), jnp.int32(0)
        for k in range(BLK):
            hit = (owners[k] == me) & (slots[k] == s)
            row = jnp.where(hit, row_ref[0, k], row)
            filled = jnp.where(hit, jnp.int32(1), filled)
        found.append((row, filled))
    return found


def entry_of_blocks(owner_ref, row_ref, me):
    owners, slots = slot_of_entry(owner_ref)
    found = []
    for b in range(BLK):
        mine, slot = jnp.int32(0), jnp.int32(0)
        for k in range(BLK):
            hit = row_ref[0, k] == b
            mine = jnp.where(hit & (owners[k] == me), jnp.int32(1), mine)
            slot = jnp.where(hit, slots[k], slot)
        found.append((mine, slot))
    return found


def thirds(x):
    parts = []
    for _ in range(3):
        part = x.astype(BF16).astype(F32)
        parts.append(part)
        x = x - part
    return parts


def product_kernel(
    owner_ref, row_ref, g_ref, o_ref, lroot_ref, rroot_ref, moment_ref, _,
    mine_ref, send_ref, psq_ref, hi_ref, lo_ref, sq_ref, rs_ref, colsum_ref, flag_ref, tick_ref, prod_ref,
):
    me = lax.axis_index("dp")
    tick_ref[...] = jnp.zeros((1, 128), F32)
    pieces = []
    for s, (row, filled) in enumerate(rows_of_slots(owner_ref, row_ref, me)):
        flag_ref[8 + s : 9 + s, :] = jnp.full((1, 128), filled, jnp.int32).astype(F32)
        rows = pl.ds(pl.multiple_of(row * B, B), B)
        block = scaled_sum(g_ref[rows, :], o_ref[rows, :])
        high = block.astype(BF16)
        hi_ref[s] = high
        lo_ref[s] = (block - high.astype(F32)).astype(BF16)
        half = jnp.dot(lroot_ref[s], high, preferred_element_type=F32).astype(BF16)
        prod = jnp.dot(half, rroot_ref[s], preferred_element_type=F32)
        prod_ref[s] = prod.astype(BF16)
        square = jnp.sum(lanes_sum(prod * prod), axis=0, keepdims=True)
        psq_ref[s : s + 1, :] = square
        pieces += thirds(jnp.concatenate([square] * 4, axis=1))
    own = entry_of_blocks(owner_ref, row_ref, me)
    at_one = me == 1
    for i in range(2):
        rows = pl.ds(pl.multiple_of((me + i) * B, B), B)
        s = scaled_sum(g_ref[rows, :], o_ref[rows, :])
        s = s * s
        sq_ref[i] = s
        rs_ref[i] = jnp.broadcast_to(jnp.sum(lanes_sum(s), axis=1, keepdims=True), (B, 128))
        colsum_ref[i : i + 1, :] = jnp.sum(s, axis=0, keepdims=True)
        for k in range(2):
            flag = jnp.where(at_one, own[i + 1][k], own[i][k])
            flag_ref[4 * k + i : 4 * k + i + 1, :] = jnp.full((1, 128), flag, jnp.int32).astype(F32)
    pieces += thirds(moment_ref[...]) + [jnp.zeros((TAIL - 18, B), F32)]
    send_ref[BLK * HALF :, :] = jnp.concatenate(pieces, axis=0).astype(BF16)
    for out, home in ((mine_ref, me), (send_ref, 1 - me)):
        for j in range(BLK):
            chunk = 3 * home + j
            block = lax.shift_right_logical(chunk, 1)
            slot = jnp.where(block == 0, own[0][1], jnp.where(block == 1, own[1][1], own[2][1]))
            rows = pl.ds(pl.multiple_of((chunk - 2 * block) * HALF, HALF), HALF)
            out[j * HALF : (j + 1) * HALF, :] = prod_ref[slot, rows, :]


def products(owner, row_block, g, o, lroot, rroot, moments, after):
    return pl.pallas_call(
        product_kernel,
        out_shape=(
            pltpu.VMEM((BLK * HALF, B), BF16),
            pltpu.VMEM((BLK * HALF + TAIL, B), BF16),
            pltpu.VMEM((CAP, 128), F32),
            pltpu.VMEM((CAP, B, B), BF16),
            pltpu.VMEM((CAP, B, B), BF16),
            pltpu.VMEM((2, B, B), F32),
            pltpu.VMEM((2, B, 128), F32),
            pltpu.VMEM((2, B), F32),
            pltpu.VMEM((16, 128), F32),
            pltpu.VMEM((1, 128), F32),
        ),
        in_specs=[SM, SM] + [VM] * 6,
        out_specs=(VM,) * 10,
        scratch_shapes=[pltpu.VMEM((CAP, B, B), BF16)],
        compiler_params=pltpu.CompilerParams(vmem_limit_bytes=12 * MIB),
        cost_estimate=pl.CostEstimate(
            flops=100 * B * B * B, bytes_accessed=8 * MIB, transcendentals=0
        ),
        name="products",
    )(owner, row_block, g, o, lroot, rroot, moments, after)


NT = (((1,), (1,)), ((), ()))
TN = (((0,), (0,)), ((), ()))


def gram(x, y, dims):
    return lax.dot_general(x, y, dims, preferred_element_type=F32)


def gram_kernel(
    hi_ref, lo_ref, _, gl_ref, gr_ref, vec_ref, tick_ref, cross_ref,
):
    tick_ref[...] = jnp.zeros((1, 128), F32)
    stats = ((gl_ref, NT), (gr_ref, TN))
    for s in range(CAP):
        hi, lo = hi_ref[s], lo_ref[s]
        for i, (out, dims) in enumerate(stats):
            cross_ref[2 * s + i] = gram(hi, lo, dims)
            out[s] = gram(hi, hi, dims)
    diagonal = lax.broadcasted_iota(jnp.int32, (128, 128), 0) == lax.broadcasted_iota(
        jnp.int32, (128, 128), 1
    )
    for s in range(CAP):
        for i, (out, _) in enumerate(stats):
            out[s] = out[s] + cross_ref[2 * s + i] + cross_ref[2 * s + i].T
            for p in range(4):
                at = slice(128 * p, 128 * (p + 1))
                line = jnp.where(diagonal, out[s, at, at], 0.0)
                vec_ref[2 * i + s : 2 * i + s + 1, at] = jnp.sum(line, axis=0, keepdims=True)


def grams(hi, lo, after):
    return pl.pallas_call(
        gram_kernel,
        out_shape=(
            pltpu.VMEM((CAP, B, B), F32),
            pltpu.VMEM((CAP, B, B), F32),
            pltpu.VMEM((4, B), F32),
            pltpu.VMEM((1, 128), F32),
        ),
        in_specs=[VM] * 3,
        out_specs=(VM,) * 4,
        scratch_shapes=[pltpu.VMEM((2 * CAP, B, B), F32)],
        compiler_params=pltpu.CompilerParams(vmem_limit_bytes=12 * MIB),
        cost_estimate=pl.CostEstimate(
            flops=400 * B * B * B, bytes_accessed=12 * MIB, transcendentals=0
        ),
        name="grams",
    )(hi, lo, after)


def finish_kernel(
    total_ref, gl_ref, gr_ref, sq_ref, rs_ref, colsum_ref, vec_ref, flag_ref,
    left_ref, right_ref, moment_ref, mine_ref, recv_ref, psq_ref,
    dir_hbm, nl_hbm, nr_hbm, nrows_hbm, ncols_hbm,
    nl_ref, nr_ref, dir_ref, nrows_ref, ncols_ref, sems, *, entries
):
    me = lax.axis_index("dp")
    total = jnp.sum(total_ref[...].reshape(-1, 128), axis=0, keepdims=True)
    total = jnp.sum(total, axis=1, keepdims=True)
    clip = lax.rsqrt(total * (1.0 / entries) + 1e-6) * (1.0 / SCALE)
    clip2 = clip * clip
    mix = (1.0 - DECAY) / B * clip2
    copies = []

    def send_out(src, dst, sem):
        copies.append(pltpu.make_async_copy(src, dst, sems.at[sem]))
        copies[-1].start()

    for s in range(CAP):
        filled = flag_ref[8 + s : 9 + s, 0:1]
        keep = 1.0 - (1.0 - DECAY) * filled
        add = mix * filled
        nrows_ref[s : s + 1, :] = keep * moment_ref[s : s + 1, :] + add * vec_ref[s : s + 1, :]
        ncols_ref[s : s + 1, :] = keep * moment_ref[2 + s : 3 + s, :] + add * vec_ref[2 + s : 3 + s, :]
        for i, (new, old, stat, hbm) in enumerate(
            ((nl_ref, left_ref, gl_ref, nl_hbm), (nr_ref, right_ref, gr_ref, nr_hbm))
        ):
            for h in range(4):
                rows = slice(h * 128, (h + 1) * 128)
                new[s, rows, :] = keep * old[s, rows, :] + add * stat[s, rows, :]
                send_out(new.at[s, rows, :], hbm.at[s, rows, :], 8 * s + 4 * i + h)
    send_out(nrows_ref, nrows_hbm, 16)
    send_out(ncols_ref, ncols_hbm, 17)
    factors, owns = [], []
    tail = recv_ref[BLK * HALF :, :].astype(F32)
    others = tail[6:10] + tail[10:14] + tail[14:18]
    for i in range(2):
        own = flag_ref[i : i + 1, 0:1] > 0.5
        first = flag_ref[4 + i : 5 + i, 0:1] < 0.5

        def pick(mine, theirs, k):
            return jnp.where(
                own,
                jnp.where(first, mine[k : k + 1, :], mine[k + 1 : k + 2, :]),
                jnp.where(first, theirs[k : k + 1, :], theirs[k + 1 : k + 2, :]),
            )

        old_rows = jnp.broadcast_to(pick(moment_ref, others, 0), (128, B)).T
        new_rows = DECAY * old_rows + mix * rs_ref[i]
        mean = jnp.sum(new_rows, axis=0, keepdims=True) * (1.0 / B)
        share = new_rows * (1.0 / mean)
        u = share * lax.rsqrt(share)
        v = jnp.sqrt(DECAY * pick(moment_ref, others, 2) + mix * colsum_ref[i : i + 1, :])
        acc = jnp.zeros((8, 128), F32)
        for j in range(4):
            cols = slice(128 * j, 128 * (j + 1))
            r = pl.reciprocal(u * v[:, cols] + 1e-8, approx=True)
            acc = acc + jnp.sum((sq_ref[i, :, cols] * r * r).reshape(B // 8, 8, 128), axis=0)
        adam = jnp.sum(jnp.sum(acc, axis=0, keepdims=True), axis=1, keepdims=True)
        adam = adam * clip2 * (1.0 / (B * B))
        theirs = jnp.concatenate(
            [tail[0:1] + tail[1:2] + tail[2:3], tail[3:4] + tail[4:5] + tail[5:6]], axis=0
        )
        psq = pick(psq_ref, theirs[:, 0:128], 0)
        psq = jnp.sum(psq, axis=1, keepdims=True) * clip2 * (1.0 / (B * B))
        factors.append(-clip * jnp.sqrt(adam) * lax.rsqrt(psq + 1e-6))
        owns.append(flag_ref[i : i + 1, 0:1])
    at_one = me == 1
    for j in range(BLK):
        rows = slice(j * HALF, (j + 1) * HALF)
        low, high = j // 2, (j + 1) // 2
        factor = jnp.where(at_one, factors[high], factors[low])
        own = jnp.where(at_one, owns[high], owns[low])
        piece = jnp.where(own > 0.5, mine_ref[rows, :].astype(F32), recv_ref[rows, :].astype(F32))
        dir_ref[rows, :] = (piece * factor).astype(BF16)
        send_out(dir_ref.at[rows, :], dir_hbm.at[rows, :], 18 + j)
    for c in copies:
        c.wait()


def finish(entries, *args):
    return pl.pallas_call(
        functools.partial(finish_kernel, entries=entries),
        out_shape=(
            jax.ShapeDtypeStruct((BLK * HALF, B), BF16),
            jax.ShapeDtypeStruct((CAP, B, B), F32),
            jax.ShapeDtypeStruct((CAP, B, B), F32),
            jax.ShapeDtypeStruct((CAP, B), F32),
            jax.ShapeDtypeStruct((CAP, B), F32),
        ),
        in_specs=[VM] * 14,
        out_specs=(HB,) * 5,
        scratch_shapes=[
            pltpu.VMEM((CAP, B, B), F32),
            pltpu.VMEM((CAP, B, B), F32),
            pltpu.VMEM((BLK * HALF, B), BF16),
            pltpu.VMEM((CAP, B), F32),
            pltpu.VMEM((CAP, B), F32),
            pltpu.SemaphoreType.DMA((21,)),
        ],
        compiler_params=pltpu.CompilerParams(vmem_limit_bytes=12 * MIB),
        cost_estimate=pl.CostEstimate(
            flops=16 * B * B, bytes_accessed=16 * MIB, transcendentals=0
        ),
        name="finish",
    )(*args)


def around(c, odd, size):
    return (((c + odd) ^ 1) - odd) % size


ROUNDS = (
    lambda z, y, x: (z, y, around(x, 0, 4)),
    lambda z, y, x: (z, y, around(x, 1, 4)),
)


def chip(z, y, x):
    return (z * 4 + y) * 4 + x


def mp_swap(v, peer):
    size = lax.axis_size("mp")
    pairs = [
        (chip(z, y, x), chip(*peer(z, y, x)))
        for z in range(8) for y in range(4) for x in range(4)
    ]
    return v + lax.ppermute(v, "mp", [p for p in pairs if max(p) < size])


def rest_chips(v):
    if lax.axis_size("mp") != 128:
        return v
    groups = [[chip(z, y, x) for z in range(8) for y in range(4)] for x in range(4)]
    many = jnp.broadcast_to(v, (len(groups[0]), 128))
    return lax.all_to_all(many, "mp", 0, 0, tiled=True, axis_index_groups=groups)


def on_device(
    grad_parts, owner, row_block, left_stats, right_stats, left_root, right_root, row_moment, col_moment
):
    entries = BLK * B * B * lax.axis_size("mp")
    o = lax.ppermute(grad_parts[0], "dp", SWAP)
    g, lroot, rroot, left, right, moments = load(
        grad_parts[0], left_root[0], right_root[0], left_stats[0], right_stats[0], row_moment[0], col_moment[0]
    )
    part = square_sum(g, o)
    mine, send, psq, hi, lo, sq, rs, colsum, flag, tick = products(owner, row_block, g, o, lroot, rroot, moments, part)
    recv = lax.ppermute(send, "dp", SWAP)
    part = mp_swap(part, ROUNDS[0]) + tick
    gl, gr, vec, tick = grams(hi, lo, part)
    part = mp_swap(part, ROUNDS[1]) + tick
    total = rest_chips(part)
    direction, new_left, new_right, new_rows, new_cols = finish(
        entries, total, gl, gr, sq, rs, colsum, vec, flag, left, right, moments, mine, recv, psq
    )
    return (direction, new_left[None], new_right[None], new_rows[None], new_cols[None])


def solution(mesh):
    return jax.shard_map(
        on_device,
        mesh=mesh,
        in_specs=(
            P("dp", None, "mp"),
            P("mp", None),
            P("mp", None),
            P("mp", "dp", None, None),
            P("mp", "dp", None, None),
            P("mp", "dp", None, None),
            P("mp", "dp", None, None),
            P("mp", "dp", None),
            P("mp", "dp", None),
        ),
        out_specs=(
            P("dp", "mp"),
            P("mp", "dp", None, None),
            P("mp", "dp", None, None),
            P("mp", "dp", None),
            P("mp", "dp", None),
        ),
        check_vma=False,
    )
```

time: 39.6 us -> 37.3 us (0.942)
  Pallas kernels: 13.5 us -> 11.5 us
    pallas_call x1, Pallas kernels: 3.82 us -> 2.4 us  [grams(): pl.pallas_call(gram_kernel, out_shape=(pltpu.VMEM((CAP, B, B), F32), pltp...]
    pallas_call x1, Pallas kernels: 3.3 us -> 2.8 us  [finish(): pl.pallas_call(functools.partial(finish_kernel, entries=entries), out_sha...]
  transfers between devices with their start and end apart: 5 -> 4, of which waited for: 0 -> 0; matrix products, arithmetic and copies ran while one was open for 0% -> 0% of each run, Pallas kernels for 26% -> 22%
where the time goes in v2:
time: 37.3 us; the launch traced here: 37.1 us
  blocking collectives  19.6 us (53%)
  Pallas kernels  11.5 us (31%)
  starting transfers between devices  5.2 us (14%)
  between operations  0.73 us (2%)
    all_to_all x1, blocking collectives, rest_chips(): lax.all_to_all(many, 'mp', 0, 0, tiled=True, axis_index_groups=groups)  19.6 us
    pallas_call x1, Pallas kernels, load(): pl.pallas_call(load_kernel, out_shape=(pltpu.VMEM((BLK * B, B), BF16), pl...  3.41 us
    ppermute x1, starting transfers between devices, on_device(): o = lax.ppermute(grad_parts[0], 'dp', SWAP)  3.33 us
    pallas_call x1, Pallas kernels, finish(): pl.pallas_call(functools.partial(finish_kernel, entries=entries), out_sha...  2.8 us
    pallas_call x1, Pallas kernels, grams(): pl.pallas_call(gram_kernel, out_shape=(pltpu.VMEM((CAP, B, B), F32), pltp...  2.4 us
    pallas_call x1, Pallas kernels, products(): pl.pallas_call(product_kernel, out_shape=(pltpu.VMEM((BLK * HALF, B), BF1...  2.37 us
    ppermute x2, starting transfers between devices, mp_swap(): return v + lax.ppermute(v, 'mp', [p for p in pairs if max(p) < size])  1.62 us
  transfers between devices with their start and end apart: 4, of which 0 were waited for; matrix products, arithmetic and copies ran while one was open for 0% of the time, Pallas kernels for 22%

profile of v2, /device:TPU:1, one launch (start us, length us, event | category | flops | bytes accessed | tf_op | source)
XLA Modules:
  0.0 37.1 jit_solution(18014176243290050381)
XLA Ops:
  0.6 3.3 %collective-permute-start = (bf16[1536,512]{1,0:T(8,128)(2,1)}, bf16[1536,512]{1,0:T(8,128)(2,1)S(1)}, u32[]{:S(2)}, u32[]{:S(2)}) collective-permute-start(bf16[1536,512]{1,0:T(8,128)(2,1)} %bitcast.17), channel_id=1, source_target_pairs={{0,128},{128,0},{1,129},{129,1},{2,130},{130,2},{3,131},{131,3},{4... | collective-permute-start | bytes 4718600 | tf_op jit(solution)/shard_map/ppermute | solution.py:406
  4.0 3.4 %load.1 = (bf16[1536,512]{1,0:T(8,128)(2,1)S(1)}, bf16[2,512,512]{2,1,0:T(8,128)(2,1)S(1)}, bf16[2,512,512]{2,1,0:T(8,128)(2,1)S(1)}, f32[2,512,512]{2,1,0:T(8,1...) custom-call(bf16[1536,512]{1,0:T(8,128)(2,1)} %bitcast.18, bf16[2,512,512]{2,1,0:T(8,128)(2,1)} %bitcast.19, ...), custom_call_target="tpu_custom_call" | custom-call | bytes 8388608 | tf_op jit(solution)/shard_map/load/pallas_call | solution.py:77
  7.4 0.0 copy-start
  7.4 0.0 copy-start.1
  7.4 0.0 collective-permute-done.o_ref
  7.4 0.6 %squares.1._ = f32[1,128]{1,0:T(1,128)S(1)} custom-call(bf16[1536,512]{1,0:T(8,128)(2,1)S(1)} %get-tuple-element.30.g_ref, bf16[1536,512]{1,0:T(8,128)(2,1)S(1)} %collective-permute-done.o_ref), custom_call_target="tpu_custom_call" | custom-call | flops 3145728 | bytes 3145728 | tf_op jit(solution)/shard_map/squares/pallas_call | solution.py:48
  8.0 0.1 collective-permute-start.1
  8.1 0.0 copy-done
  8.1 0.0 copy-done.1
  8.1 2.4 %products.1 = (bf16[768,512]{1,0:T(8,128)(2,1)S(1)}, bf16[800,512]{1,0:T(8,128)(2,1)S(1)}, f32[2,128]{1,0:T(2,128)S(1)}, bf16[2,512,512]{2,1,0:T(8,128)(2,1)S(1)...) custom-call(s32[1,3]{1,0:T(1,128)S(1)} %copy-done, ...), custom_call_target="tpu_custom_call" | custom-call | flops 13421772800 | bytes 8388608 | tf_op jit(solution)/shard_map/products/pallas_call | solution.py:188
  10.5 0.3 collective-permute-start.3
  10.7 0.0 collective-permute-done.1
  10.7 1.5 %collective-permute-start.2 = (f32[1,128]{1,0:T(1,128)S(1)}, f32[1,128]{1,0:T(1,128)S(1)}, u32[]{:S(2)}, u32[]{:S(2)}) collective-permute-start(f32[1,128]{1,0:T(1,128)S(1)} %add_add_fusion._), channel_id=1, source_target_pairs={{0,3},{1,2},{2,1},{3,0},{4,7},{5,6},{6,5},{7,4},{8,11},{9,10},{10,... | collective-permute-start | bytes 1544 | tf_op jit(solution)/shard_map/ppermute | solution.py:391
  12.3 2.4 %grams.1 = (f32[2,512,512]{2,1,0:T(8,128)S(1)}, f32[2,512,512]{2,1,0:T(8,128)S(1)}, f32[4,512]{1,0:T(4,128)S(1)}, f32[1,128]{1,0:T(1,128)S(1)}) custom-call(bf16[2,512,512]{2,1,0:T(8,128)(2,1)S(1)} %get-tuple-element.35.hi_ref, bf16[2,512,512]{2,1,0:T(8,128)(2,1)S(1)} %get-tuple-element.36.lo_ref, f32[1,128]{1,0:T(1,128)S(1)} %add_add_fusion._), custom_call_target="tpu_custom_call" | custom-call | flops 53687091200 | bytes 12582912 | tf_op jit(solution)/shard_map/grams/pallas_call | solution.py:244
  14.7 0.0 collective-permute-done.2
  14.7 19.6 %all_to_all.8 = f32[32,1,128]{2,1,0:T(1,128)S(1)} all-to-all(f32[32,1,128]{2,1,0:T(1,128)S(1)} %broadcast_in_dim.17), channel_id=1, replica_groups={{0,4,8,12,16,20,24,28,32,36,40,44,48,52,56,60,64,68,72,76,80,84,88,92,9..., dimensions={0} | all-to-all | bytes 32768 | tf_op jit(solution)/shard_map/all_to_all | solution.py:399
  34.3 0.0 collective-permute-done.3.recv_ref
  34.3 2.8 %finish.1 = (bf16[768,512]{1,0:T(8,128)(2,1)}, f32[2,512,512]{2,1,0:T(8,128)}, f32[2,512,512]{2,1,0:T(8,128)}, f32[2,512]{1,0:T(2,128)}, f32[2,512]{1,0:T(2,128)}) custom-call(f32[32,128]{1,0:T(8,128)S(1)} %bitcast.14, f32[2,512,512]{2,1,0:T(8,128)S(1)} %get-tuple-element.38.gl_ref, f32[2,512,512]{2,1,0:T(8,128)S(1)} %get-tuple-element.39.gr_ref, ...), custom_call_target="tpu_custom_call" | custom-call | flops 4194304 | bytes 16777216 | tf_op jit(solution)/shard_map/finish/pallas_call | solution.py:344
  (3 shorter events, 0.0 us)
Async XLA Ops:
  0.6 6.8 %collective-permute-start = (bf16[1536,512]{1,0:T(8,128)(2,1)}, bf16[1536,512]{1,0:T(8,128)(2,1)S(1)}, u32[]{:S(2)}, u32[]{:S(2)}) collective-permute-start(bf16[1536,512]{1,0:T(8,128)(2,1)} %bitcast.17), channel_id=1, source_target_pairs={{0,128},{128,0},{1,129},{129,1},{2,130},{130,2},{3,131},{131,3},{4... | collective-permute-start | bytes 4718600 | tf_op jit(solution)/shard_map/ppermute | solution.py:406
  7.4 0.7 %copy-start = (s32[1,3]{1,0:T(1,128)S(1)}, s32[1,3]{1,0:T(1,128)}, u32[]{:S(2)}) copy-start(s32[1,3]{1,0:T(1,128)} %owner_ref.1) | copy-start | bytes 40
  7.4 0.7 %copy-start.1 = (s32[1,3]{1,0:T(1,128)S(1)}, s32[1,3]{1,0:T(1,128)}, u32[]{:S(2)}) copy-start(s32[1,3]{1,0:T(1,128)} %row_ref.1) | copy-start | bytes 40
  8.0 2.7 %collective-permute-start.1 = (f32[1,128]{1,0:T(1,128)S(1)}, f32[1,128]{1,0:T(1,128)S(1)}, u32[]{:S(2)}, u32[]{:S(2)}) collective-permute-start(f32[1,128]{1,0:T(1,128)S(1)} %squares.1._), channel_id=1, source_target_pairs={{0,1},{1,0},{2,3},{3,2},{4,5},{5,4},{6,7},{7,6},{8,9},{9,8},{10,11... | collective-permute-start | bytes 1544 | tf_op jit(solution)/shard_map/ppermute | solution.py:391
  10.5 23.8 %collective-permute-start.3 = (bf16[800,512]{1,0:T(8,128)(2,1)S(1)}, bf16[800,512]{1,0:T(8,128)(2,1)S(1)}, u32[]{:S(2)}, u32[]{:S(2)}) collective-permute-start(bf16[800,512]{1,0:T(8,128)(2,1)S(1)} %get-tuple-element.48), channel_id=1, source_target_pairs={{0,128},{128,0},{1,129},{129,1},{2,130},{130,2},{3,131},{131,3},{4... | collective-permute-start | bytes 2457608 | tf_op jit(solution)/shard_map/ppermute | solution.py:412
  10.7 3.9 %collective-permute-start.2 = (f32[1,128]{1,0:T(1,128)S(1)}, f32[1,128]{1,0:T(1,128)S(1)}, u32[]{:S(2)}, u32[]{:S(2)}) collective-permute-start(f32[1,128]{1,0:T(1,128)S(1)} %add_add_fusion._), channel_id=1, source_target_pairs={{0,3},{1,2},{2,1},{3,0},{4,7},{5,6},{6,5},{7,4},{8,11},{9,10},{10,... | collective-permute-start | bytes 1544 | tf_op jit(solution)/shard_map/ppermute | solution.py:391

commit v3 on v2

--- a/solution.py
+++ b/solution.py
@@ -59,25 +59,44 @@
 
 
 def load_kernel(g_hbm, lroot_hbm, rroot_hbm, left_hbm, right_hbm, rows_hbm, cols_hbm,
-                g_ref, lroot_ref, rroot_ref, left_ref, right_ref, moment_ref, rows_ref, cols_ref, sems):
-    pairs = (
-        (rows_hbm, rows_ref), (cols_hbm, cols_ref), (g_hbm, g_ref), (lroot_hbm, lroot_ref), (rroot_hbm, rroot_ref),
-        (left_hbm, left_ref), (right_hbm, right_ref),
-    )
+                g_ref, lroot_ref, rroot_ref, left_ref, right_ref, moment_ref, part_ref, rows_ref, cols_ref, sems):
+    pairs = [
+        (g_hbm, part_ref), (rows_hbm, rows_ref), (cols_hbm, cols_ref),
+        (left_hbm.at[0], left_ref.at[0]), (right_hbm.at[0], right_ref.at[0]),
+        (lroot_hbm, lroot_ref), (rroot_hbm, rroot_ref),
+        (left_hbm.at[1], left_ref.at[1]), (right_hbm.at[1], right_ref.at[1]),
+    ]
     copies = [pltpu.make_async_copy(a, b, sems.at[i]) for i, (a, b) in enumerate(pairs)]
     for c in copies:
         c.start()
-    for c in copies:
+    copies[0].wait()
+    step = 64
+
+    def widen(i, carry):
+        rows = pl.ds(pl.multiple_of(i * step, step), step)
+        g_ref[rows, :] = part_ref[rows, :].astype(F32)
+        return carry
+
+    lax.fori_loop(0, BLK * B // step, widen, 0, unroll=4)
+    for c in copies[1:5]:
         c.wait()
     moment_ref[0:2, :] = rows_ref[...]
     moment_ref[2:4, :] = cols_ref[...]
+    left_ref[0] = left_ref[0] * DECAY
+    right_ref[0] = right_ref[0] * DECAY
+    for c in copies[5:]:
+        c.wait()
+
+
+def in_hbm(*arrays):
+    return [pltpu.with_memory_space_constraint(a, pltpu.HBM) for a in arrays]
 
 
 def load(g, lroot, rroot, left, right, rows, cols):
     return pl.pallas_call(
         load_kernel,
         out_shape=(
-            pltpu.VMEM((BLK * B, B), BF16),
+            pltpu.VMEM((BLK * B, B), F32),
             pltpu.VMEM((CAP, B, B), BF16),
             pltpu.VMEM((CAP, B, B), BF16),
             pltpu.VMEM((CAP, B, B), F32),
@@ -87,14 +106,15 @@
         in_specs=[HB] * 7,
         out_specs=(VM,) * 6,
         scratch_shapes=[
+            pltpu.VMEM((BLK * B, B), BF16),
             pltpu.VMEM((CAP, B), F32),
             pltpu.VMEM((CAP, B), F32),
-            pltpu.SemaphoreType.DMA((7,)),
+            pltpu.SemaphoreType.DMA((9,)),
         ],
-        compiler_params=pltpu.CompilerParams(vmem_limit_bytes=2 * MIB),
+        compiler_params=pltpu.CompilerParams(vmem_limit_bytes=4 * MIB),
         cost_estimate=pl.CostEstimate(flops=0, bytes_accessed=8 * MIB, transcendentals=0),
         name="load",
-    )(*[pltpu.with_memory_space_constraint(a, pltpu.HBM) for a in (g, lroot, rroot, left, right, rows, cols)])
+    )(*in_hbm(g, lroot, rroot, left, right, rows, cols))
 
 
 def slot_of_entry(owner_ref):
@@ -289,7 +309,8 @@
         ):
             for h in range(4):
                 rows = slice(h * 128, (h + 1) * 128)
-                new[s, rows, :] = keep * old[s, rows, :] + add * stat[s, rows, :]
+                kept = old[s, rows, :] if s == 0 else keep * old[s, rows, :]
+                new[s, rows, :] = kept + add * stat[s, rows, :]
                 send_out(new.at[s, rows, :], hbm.at[s, rows, :], 8 * s + 4 * i + h)
     send_out(nrows_ref, nrows_hbm, 16)
     send_out(ncols_ref, ncols_hbm, 17)

time: 37.3 us -> 37.1 us (level)
  no operation moved by 1% of the time
where the time goes in v3:
time: 37.1 us; the launch traced here: 37 us
  blocking collectives  19.6 us (53%)
  Pallas kernels  11.4 us (31%)
  starting transfers between devices  5.19 us (14%)
  between operations  0.72 us (2%)
    all_to_all x1, blocking collectives, rest_chips(): lax.all_to_all(many, 'mp', 0, 0, tiled=True, axis_index_groups=groups)  19.6 us
    pallas_call x1, Pallas kernels, load(): pl.pallas_call(load_kernel, out_shape=(pltpu.VMEM((BLK * B, B), F32), plt...  3.36 us
    ppermute x1, starting transfers between devices, on_device(): o = lax.ppermute(grad_parts[0], 'dp', SWAP)  3.33 us
    pallas_call x1, Pallas kernels, finish(): pl.pallas_call(functools.partial(finish_kernel, entries=entries), out_sha...  2.78 us
    pallas_call x1, Pallas kernels, grams(): pl.pallas_call(gram_kernel, out_shape=(pltpu.VMEM((CAP, B, B), F32), pltp...  2.52 us
    pallas_call x1, Pallas kernels, products(): pl.pallas_call(product_kernel, out_shape=(pltpu.VMEM((BLK * HALF, B), BF1...  2.26 us
    ppermute x2, starting transfers between devices, mp_swap(): return v + lax.ppermute(v, 'mp', [p for p in pairs if max(p) < size])  1.54 us
  transfers between devices with their start and end apart: 4, of which 0 were waited for; matrix products, arithmetic and copies ran while one was open for 0% of the time, Pallas kernels for 22%

profile of v3, /device:TPU:1, one launch (start us, length us, event | category | flops | bytes accessed | tf_op | source)
XLA Modules:
  0.0 37.0 jit_solution(14818230020167229735)
XLA Ops:
  0.6 3.3 %collective-permute-start = (bf16[1536,512]{1,0:T(8,128)(2,1)}, bf16[1536,512]{1,0:T(8,128)(2,1)S(1)}, u32[]{:S(2)}, u32[]{:S(2)}) collective-permute-start(bf16[1536,512]{1,0:T(8,128)(2,1)} %bitcast.17), channel_id=1, source_target_pairs={{0,128},{128,0},{1,129},{129,1},{2,130},{130,2},{3,131},{131,3},{4... | collective-permute-start | bytes 4718600 | tf_op jit(solution)/shard_map/ppermute | solution.py:427
  4.0 3.4 %load.1 = (f32[1536,512]{1,0:T(8,128)S(1)}, bf16[2,512,512]{2,1,0:T(8,128)(2,1)S(1)}, bf16[2,512,512]{2,1,0:T(8,128)(2,1)S(1)}, f32[2,512,512]{2,1,0:T(8,128)S(1...) custom-call(bf16[1536,512]{1,0:T(8,128)(2,1)} %bitcast.18, bf16[2,512,512]{2,1,0:T(8,128)(2,1)} %bitcast.19, ...), custom_call_target="tpu_custom_call" | custom-call | bytes 8388608 | tf_op jit(solution)/shard_map/load/pallas_call | solution.py:96
  7.3 0.0 collective-permute-done.o_ref
  7.3 0.0 copy-start
  7.3 0.0 copy-start.1
  7.4 0.4 %squares.1._ = f32[1,128]{1,0:T(1,128)S(1)} custom-call(f32[1536,512]{1,0:T(8,128)S(1)} %get-tuple-element.30.g_ref, bf16[1536,512]{1,0:T(8,128)(2,1)S(1)} %collective-permute-done.o_ref), custom_call_target="tpu_custom_call" | custom-call | flops 3145728 | bytes 3145728 | tf_op jit(solution)/shard_map/squares/pallas_call | solution.py:48
  7.8 0.1 collective-permute-start.1
  7.9 0.1 copy-done
  8.0 0.0 copy-done.1
  8.0 2.3 %products.1 = (bf16[768,512]{1,0:T(8,128)(2,1)S(1)}, bf16[800,512]{1,0:T(8,128)(2,1)S(1)}, f32[2,128]{1,0:T(2,128)S(1)}, bf16[2,512,512]{2,1,0:T(8,128)(2,1)S(1)...) custom-call(s32[1,3]{1,0:T(1,128)S(1)} %copy-done, ...), custom_call_target="tpu_custom_call" | custom-call | flops 13421772800 | bytes 8388608 | tf_op jit(solution)/shard_map/products/pallas_call | solution.py:208
  10.3 0.3 collective-permute-start.3
  10.6 0.0 collective-permute-done.1
  10.6 1.4 %collective-permute-start.2 = (f32[1,128]{1,0:T(1,128)S(1)}, f32[1,128]{1,0:T(1,128)S(1)}, u32[]{:S(2)}, u32[]{:S(2)}) collective-permute-start(f32[1,128]{1,0:T(1,128)S(1)} %add_add_fusion._), channel_id=1, source_target_pairs={{0,3},{1,2},{2,1},{3,0},{4,7},{5,6},{6,5},{7,4},{8,11},{9,10},{10,... | collective-permute-start | bytes 1544 | tf_op jit(solution)/shard_map/ppermute | solution.py:412
  12.1 2.5 %grams.1 = (f32[2,512,512]{2,1,0:T(8,128)S(1)}, f32[2,512,512]{2,1,0:T(8,128)S(1)}, f32[4,512]{1,0:T(4,128)S(1)}, f32[1,128]{1,0:T(1,128)S(1)}) custom-call(bf16[2,512,512]{2,1,0:T(8,128)(2,1)S(1)} %get-tuple-element.35.hi_ref, bf16[2,512,512]{2,1,0:T(8,128)(2,1)S(1)} %get-tuple-element.36.lo_ref, f32[1,128]{1,0:T(1,128)S(1)} %add_add_fusion._), custom_call_target="tpu_custom_call" | custom-call | flops 53687091200 | bytes 12582912 | tf_op jit(solution)/shard_map/grams/pallas_call | solution.py:264
  14.6 0.0 collective-permute-done.2
  14.6 19.6 %all_to_all.8 = f32[32,1,128]{2,1,0:T(1,128)S(1)} all-to-all(f32[32,1,128]{2,1,0:T(1,128)S(1)} %broadcast_in_dim.17), channel_id=1, replica_groups={{0,4,8,12,16,20,24,28,32,36,40,44,48,52,56,60,64,68,72,76,80,84,88,92,9..., dimensions={0} | all-to-all | bytes 32768 | tf_op jit(solution)/shard_map/all_to_all | solution.py:420
  34.2 0.0 collective-permute-done.3.recv_ref
  34.2 2.8 %finish.1 = (bf16[768,512]{1,0:T(8,128)(2,1)}, f32[2,512,512]{2,1,0:T(8,128)}, f32[2,512,512]{2,1,0:T(8,128)}, f32[2,512]{1,0:T(2,128)}, f32[2,512]{1,0:T(2,128)}) custom-call(f32[32,128]{1,0:T(8,128)S(1)} %bitcast.14, f32[2,512,512]{2,1,0:T(8,128)S(1)} %get-tuple-element.38.gl_ref, f32[2,512,512]{2,1,0:T(8,128)S(1)} %get-tuple-element.39.gr_ref, ...), custom_call_target="tpu_custom_call" | custom-call | flops 4194304 | bytes 16777216 | tf_op jit(solution)/shard_map/finish/pallas_call | solution.py:365
  (3 shorter events, 0.0 us)
Async XLA Ops:
  0.6 6.7 %collective-permute-start = (bf16[1536,512]{1,0:T(8,128)(2,1)}, bf16[1536,512]{1,0:T(8,128)(2,1)S(1)}, u32[]{:S(2)}, u32[]{:S(2)}) collective-permute-start(bf16[1536,512]{1,0:T(8,128)(2,1)} %bitcast.17), channel_id=1, source_target_pairs={{0,128},{128,0},{1,129},{129,1},{2,130},{130,2},{3,131},{131,3},{4... | collective-permute-start | bytes 4718600 | tf_op jit(solution)/shard_map/ppermute | solution.py:427
  7.3 0.7 %copy-start = (s32[1,3]{1,0:T(1,128)S(1)}, s32[1,3]{1,0:T(1,128)}, u32[]{:S(2)}) copy-start(s32[1,3]{1,0:T(1,128)} %owner_ref.1) | copy-start | bytes 40
  7.3 0.7 %copy-start.1 = (s32[1,3]{1,0:T(1,128)S(1)}, s32[1,3]{1,0:T(1,128)}, u32[]{:S(2)}) copy-start(s32[1,3]{1,0:T(1,128)} %row_ref.1) | copy-start | bytes 40
  7.8 2.8 %collective-permute-start.1 = (f32[1,128]{1,0:T(1,128)S(1)}, f32[1,128]{1,0:T(1,128)S(1)}, u32[]{:S(2)}, u32[]{:S(2)}) collective-permute-start(f32[1,128]{1,0:T(1,128)S(1)} %squares.1._), channel_id=1, source_target_pairs={{0,1},{1,0},{2,3},{3,2},{4,5},{5,4},{6,7},{7,6},{8,9},{9,8},{10,11... | collective-permute-start | bytes 1544 | tf_op jit(solution)/shard_map/ppermute | solution.py:412
  10.3 23.9 %collective-permute-start.3 = (bf16[800,512]{1,0:T(8,128)(2,1)S(1)}, bf16[800,512]{1,0:T(8,128)(2,1)S(1)}, u32[]{:S(2)}, u32[]{:S(2)}) collective-permute-start(bf16[800,512]{1,0:T(8,128)(2,1)S(1)} %get-tuple-element.48), channel_id=1, source_target_pairs={{0,128},{128,0},{1,129},{129,1},{2,130},{130,2},{3,131},{131,3},{4... | collective-permute-start | bytes 2457608 | tf_op jit(solution)/shard_map/ppermute | solution.py:433
  10.6 4.0 %collective-permute-start.2 = (f32[1,128]{1,0:T(1,128)S(1)}, f32[1,128]{1,0:T(1,128)S(1)}, u32[]{:S(2)}, u32[]{:S(2)}) collective-permute-start(f32[1,128]{1,0:T(1,128)S(1)} %add_add_fusion._), channel_id=1, source_target_pairs={{0,3},{1,2},{2,1},{3,0},{4,7},{5,6},{6,5},{7,4},{8,11},{9,10},{10,... | collective-permute-start | bytes 1544 | tf_op jit(solution)/shard_map/ppermute | solution.py:412

commit v4 on v3

--- a/solution.py
+++ b/solution.py
@@ -239,50 +239,64 @@
 
 
 def gram_kernel(
-    hi_ref, lo_ref, _, gl_ref, gr_ref, vec_ref, tick_ref, cross_ref,
+    hi_ref, lo_ref, left_ref, right_ref, flag_ref, _,
+    gl_ref, gr_ref, vec_ref, left1_ref, right1_ref, tick_ref, cross_ref,
 ):
     tick_ref[...] = jnp.zeros((1, 128), F32)
     stats = ((gl_ref, NT), (gr_ref, TN))
+    halves = (slice(0, HALF), slice(HALF, B))
+    lower = ((0, 0), (1, 1), (1, 0))
     for s in range(CAP):
         hi, lo = hi_ref[s], lo_ref[s]
         for i, (out, dims) in enumerate(stats):
             cross_ref[2 * s + i] = gram(hi, lo, dims)
-            out[s] = gram(hi, hi, dims)
+            parts = [hi[h, :] if dims is NT else hi[:, h] for h in halves]
+            for p, q in lower:
+                out[s, halves[p], halves[q]] = gram(parts[p], parts[q], dims)
+    keep = 1.0 - (1.0 - DECAY) * flag_ref[9:10, 0:1]
+    left1_ref[...] = keep * left_ref[1]
+    right1_ref[...] = keep * right_ref[1]
     diagonal = lax.broadcasted_iota(jnp.int32, (128, 128), 0) == lax.broadcasted_iota(
         jnp.int32, (128, 128), 1
     )
     for s in range(CAP):
         for i, (out, _) in enumerate(stats):
-            out[s] = out[s] + cross_ref[2 * s + i] + cross_ref[2 * s + i].T
+            for p, q in lower:
+                at = (halves[p], halves[q])
+                flip = cross_ref[2 * s + i, halves[q], halves[p]].T
+                out[s, *at] = out[s, *at] + cross_ref[2 * s + i, *at] + flip
+            out[s, halves[0], halves[1]] = out[s, halves[1], halves[0]].T
             for p in range(4):
                 at = slice(128 * p, 128 * (p + 1))
                 line = jnp.where(diagonal, out[s, at, at], 0.0)
                 vec_ref[2 * i + s : 2 * i + s + 1, at] = jnp.sum(line, axis=0, keepdims=True)
 
 
-def grams(hi, lo, after):
+def grams(hi, lo, left, right, flag, after):
     return pl.pallas_call(
         gram_kernel,
         out_shape=(
             pltpu.VMEM((CAP, B, B), F32),
             pltpu.VMEM((CAP, B, B), F32),
             pltpu.VMEM((4, B), F32),
+            pltpu.VMEM((B, B), F32),
+            pltpu.VMEM((B, B), F32),
             pltpu.VMEM((1, 128), F32),
         ),
-        in_specs=[VM] * 3,
-        out_specs=(VM,) * 4,
+        in_specs=[VM] * 6,
+        out_specs=(VM,) * 6,
         scratch_shapes=[pltpu.VMEM((2 * CAP, B, B), F32)],
         compiler_params=pltpu.CompilerParams(vmem_limit_bytes=12 * MIB),
         cost_estimate=pl.CostEstimate(
             flops=400 * B * B * B, bytes_accessed=12 * MIB, transcendentals=0
         ),
         name="grams",
-    )(hi, lo, after)
+    )(hi, lo, left, right, flag, after)
 
 
 def finish_kernel(
     total_ref, gl_ref, gr_ref, sq_ref, rs_ref, colsum_ref, vec_ref, flag_ref,
-    left_ref, right_ref, moment_ref, mine_ref, recv_ref, psq_ref,
+    left_ref, right_ref, left1_ref, right1_ref, moment_ref, mine_ref, recv_ref, psq_ref,
     dir_hbm, nl_hbm, nr_hbm, nrows_hbm, ncols_hbm,
     nl_ref, nr_ref, dir_ref, nrows_ref, ncols_ref, sems, *, entries
 ):
@@ -305,12 +319,14 @@
         nrows_ref[s : s + 1, :] = keep * moment_ref[s : s + 1, :] + add * vec_ref[s : s + 1, :]
         ncols_ref[s : s + 1, :] = keep * moment_ref[2 + s : 3 + s, :] + add * vec_ref[2 + s : 3 + s, :]
         for i, (new, old, stat, hbm) in enumerate(
-            ((nl_ref, left_ref, gl_ref, nl_hbm), (nr_ref, right_ref, gr_ref, nr_hbm))
+            (
+                (nl_ref, (left_ref.at[0], left1_ref)[s], gl_ref, nl_hbm),
+                (nr_ref, (right_ref.at[0], right1_ref)[s], gr_ref, nr_hbm),
+            )
         ):
             for h in range(4):
                 rows = slice(h * 128, (h + 1) * 128)
-                kept = old[s, rows, :] if s == 0 else keep * old[s, rows, :]
-                new[s, rows, :] = kept + add * stat[s, rows, :]
+                new[s, rows, :] = old[rows, :] + add * stat[s, rows, :]
                 send_out(new.at[s, rows, :], hbm.at[s, rows, :], 8 * s + 4 * i + h)
     send_out(nrows_ref, nrows_hbm, 16)
     send_out(ncols_ref, ncols_hbm, 17)
@@ -371,7 +387,7 @@
             jax.ShapeDtypeStruct((CAP, B), F32),
             jax.ShapeDtypeStruct((CAP, B), F32),
         ),
-        in_specs=[VM] * 14,
+        in_specs=[VM] * 16,
         out_specs=(HB,) * 5,
         scratch_shapes=[
             pltpu.VMEM((CAP, B, B), F32),
@@ -432,11 +448,11 @@
     mine, send, psq, hi, lo, sq, rs, colsum, flag, tick = products(owner, row_block, g, o, lroot, rroot, moments, part)
     recv = lax.ppermute(send, "dp", SWAP)
     part = mp_swap(part, ROUNDS[0]) + tick
-    gl, gr, vec, tick = grams(hi, lo, part)
+    gl, gr, vec, left1, right1, tick = grams(hi, lo, left, right, flag, part)
     part = mp_swap(part, ROUNDS[1]) + tick
     total = rest_chips(part)
     direction, new_left, new_right, new_rows, new_cols = finish(
-        entries, total, gl, gr, sq, rs, colsum, vec, flag, left, right, moments, mine, recv, psq
+        entries, total, gl, gr, sq, rs, colsum, vec, flag, left, right, left1, right1, moments, mine, recv, psq
     )
     return (direction, new_left[None], new_right[None], new_rows[None], new_cols[None])
 

time: 37.1 us -> 36.9 us (level)
  Pallas kernels: 11.4 us -> 11 us
where the time goes in v4:
time: 36.9 us; the launch traced here: 36.6 us
  blocking collectives  19.6 us (53%)
  Pallas kernels  11 us (30%)
  starting transfers between devices  5.19 us (14%)
  between operations  0.72 us (2%)
    all_to_all x1, blocking collectives, rest_chips(): lax.all_to_all(many, 'mp', 0, 0, tiled=True, axis_index_groups=groups)  19.6 us
    pallas_call x1, Pallas kernels, load(): pl.pallas_call(load_kernel, out_shape=(pltpu.VMEM((BLK * B, B), F32), plt...  3.36 us
    ppermute x1, starting transfers between devices, on_device(): o = lax.ppermute(grad_parts[0], 'dp', SWAP)  3.33 us
    pallas_call x1, Pallas kernels, finish(): pl.pallas_call(functools.partial(finish_kernel, entries=entries), out_sha...  2.6 us
    pallas_call x1, Pallas kernels, grams(): pl.pallas_call(gram_kernel, out_shape=(pltpu.VMEM((CAP, B, B), F32), pltp...  2.29 us
    pallas_call x1, Pallas kernels, products(): pl.pallas_call(product_kernel, out_shape=(pltpu.VMEM((BLK * HALF, B), BF1...  2.26 us
    ppermute x2, starting transfers between devices, mp_swap(): return v + lax.ppermute(v, 'mp', [p for p in pairs if max(p) < size])  1.54 us
  transfers between devices with their start and end apart: 4, of which 0 were waited for; matrix products, arithmetic and copies ran while one was open for 0% of the time, Pallas kernels for 22%

profile of v4, /device:TPU:1, one launch (start us, length us, event | category | flops | bytes accessed | tf_op | source)
XLA Modules:
  0.0 36.6 jit_solution(7224611943953192866)
XLA Ops:
  0.6 3.3 %collective-permute-start = (bf16[1536,512]{1,0:T(8,128)(2,1)}, bf16[1536,512]{1,0:T(8,128)(2,1)S(1)}, u32[]{:S(2)}, u32[]{:S(2)}) collective-permute-start(bf16[1536,512]{1,0:T(8,128)(2,1)} %bitcast.17), channel_id=1, source_target_pairs={{0,128},{128,0},{1,129},{129,1},{2,130},{130,2},{3,131},{131,3},{4... | collective-permute-start | bytes 4718600 | tf_op jit(solution)/shard_map/ppermute | solution.py:443
  4.0 3.4 %load.1 = (f32[1536,512]{1,0:T(8,128)S(1)}, bf16[2,512,512]{2,1,0:T(8,128)(2,1)S(1)}, bf16[2,512,512]{2,1,0:T(8,128)(2,1)S(1)}, f32[2,512,512]{2,1,0:T(8,128)S(1...) custom-call(bf16[1536,512]{1,0:T(8,128)(2,1)} %bitcast.18, bf16[2,512,512]{2,1,0:T(8,128)(2,1)} %bitcast.19, ...), custom_call_target="tpu_custom_call" | custom-call | bytes 8388608 | tf_op jit(solution)/shard_map/load/pallas_call | solution.py:96
  7.3 0.0 collective-permute-done.o_ref
  7.3 0.0 copy-start
  7.3 0.0 copy-start.1
  7.4 0.4 %squares.1._ = f32[1,128]{1,0:T(1,128)S(1)} custom-call(f32[1536,512]{1,0:T(8,128)S(1)} %get-tuple-element.32.g_ref, bf16[1536,512]{1,0:T(8,128)(2,1)S(1)} %collective-permute-done.o_ref), custom_call_target="tpu_custom_call" | custom-call | flops 3145728 | bytes 3145728 | tf_op jit(solution)/shard_map/squares/pallas_call | solution.py:48
  7.8 0.1 collective-permute-start.1
  7.9 0.1 copy-done
  8.0 0.0 copy-done.1
  8.0 2.3 %products.1 = (bf16[768,512]{1,0:T(8,128)(2,1)S(1)}, bf16[800,512]{1,0:T(8,128)(2,1)S(1)}, f32[2,128]{1,0:T(2,128)S(1)}, bf16[2,512,512]{2,1,0:T(8,128)(2,1)S(1)...) custom-call(s32[1,3]{1,0:T(1,128)S(1)} %copy-done, ...), custom_call_target="tpu_custom_call" | custom-call | flops 13421772800 | bytes 8388608 | tf_op jit(solution)/shard_map/products/pallas_call | solution.py:208
  10.3 0.3 collective-permute-start.3
  10.6 0.0 collective-permute-done.1
  10.6 1.4 %collective-permute-start.2 = (f32[1,128]{1,0:T(1,128)S(1)}, f32[1,128]{1,0:T(1,128)S(1)}, u32[]{:S(2)}, u32[]{:S(2)}) collective-permute-start(f32[1,128]{1,0:T(1,128)S(1)} %add_add_fusion._), channel_id=1, source_target_pairs={{0,3},{1,2},{2,1},{3,0},{4,7},{5,6},{6,5},{7,4},{8,11},{9,10},{10,... | collective-permute-start | bytes 1544 | tf_op jit(solution)/shard_map/ppermute | solution.py:428
  12.1 2.3 %grams.1 = (f32[2,512,512]{2,1,0:T(8,128)S(1)}, f32[2,512,512]{2,1,0:T(8,128)S(1)}, f32[4,512]{1,0:T(4,128)S(1)}, f32[512,512]{1,0:T(8,128)S(1)}, f32[512,512]{1,0:T(8,128)S(1)}, /*index=5*/f32[1,128]{1,0:T(1,128)S(1)}) custom-call(bf16[2,512,512]{2,1,0:T(8,128)(2,1)S(1)} %get-tuple-element.37.hi_ref, bf16[2,512,512]{2,1,0:T(8,128)(2,1)S(1)} %get-tuple-element.38.lo_ref, ...), custom_call_target="tpu_custom_call" | custom-call | flops 53687091200 | bytes 12582912 | tf_op jit(solution)/shard_map/grams/pallas_call | solution.py:276
  14.4 0.0 collective-permute-done.2
  14.4 19.6 %all_to_all.8 = f32[32,1,128]{2,1,0:T(1,128)S(1)} all-to-all(f32[32,1,128]{2,1,0:T(1,128)S(1)} %broadcast_in_dim.17), channel_id=1, replica_groups={{0,4,8,12,16,20,24,28,32,36,40,44,48,52,56,60,64,68,72,76,80,84,88,92,9..., dimensions={0} | all-to-all | bytes 32768 | tf_op jit(solution)/shard_map/all_to_all | solution.py:436
  34.0 0.0 collective-permute-done.3.recv_ref
  34.0 2.6 %finish.1 = (bf16[768,512]{1,0:T(8,128)(2,1)}, f32[2,512,512]{2,1,0:T(8,128)}, f32[2,512,512]{2,1,0:T(8,128)}, f32[2,512]{1,0:T(2,128)}, f32[2,512]{1,0:T(2,128)}) custom-call(f32[32,128]{1,0:T(8,128)S(1)} %bitcast.14, f32[2,512,512]{2,1,0:T(8,128)S(1)} %get-tuple-element.43.gl_ref, f32[2,512,512]{2,1,0:T(8,128)S(1)} %get-tuple-element.44.gr_ref, ...), custom_call_target="tpu_custom_call" | custom-call | flops 4194304 | bytes 16777216 | tf_op jit(solution)/shard_map/finish/pallas_call | solution.py:381
  (3 shorter events, 0.0 us)
Async XLA Ops:
  0.6 6.7 %collective-permute-start = (bf16[1536,512]{1,0:T(8,128)(2,1)}, bf16[1536,512]{1,0:T(8,128)(2,1)S(1)}, u32[]{:S(2)}, u32[]{:S(2)}) collective-permute-start(bf16[1536,512]{1,0:T(8,128)(2,1)} %bitcast.17), channel_id=1, source_target_pairs={{0,128},{128,0},{1,129},{129,1},{2,130},{130,2},{3,131},{131,3},{4... | collective-permute-start | bytes 4718600 | tf_op jit(solution)/shard_map/ppermute | solution.py:443
  7.3 0.7 %copy-start = (s32[1,3]{1,0:T(1,128)S(1)}, s32[1,3]{1,0:T(1,128)}, u32[]{:S(2)}) copy-start(s32[1,3]{1,0:T(1,128)} %owner_ref.1) | copy-start | bytes 40
  7.3 0.7 %copy-start.1 = (s32[1,3]{1,0:T(1,128)S(1)}, s32[1,3]{1,0:T(1,128)}, u32[]{:S(2)}) copy-start(s32[1,3]{1,0:T(1,128)} %row_ref.1) | copy-start | bytes 40
  7.8 2.8 %collective-permute-start.1 = (f32[1,128]{1,0:T(1,128)S(1)}, f32[1,128]{1,0:T(1,128)S(1)}, u32[]{:S(2)}, u32[]{:S(2)}) collective-permute-start(f32[1,128]{1,0:T(1,128)S(1)} %squares.1._), channel_id=1, source_target_pairs={{0,1},{1,0},{2,3},{3,2},{4,5},{5,4},{6,7},{7,6},{8,9},{9,8},{10,11... | collective-permute-start | bytes 1544 | tf_op jit(solution)/shard_map/ppermute | solution.py:428
  10.3 23.7 %collective-permute-start.3 = (bf16[800,512]{1,0:T(8,128)(2,1)S(1)}, bf16[800,512]{1,0:T(8,128)(2,1)S(1)}, u32[]{:S(2)}, u32[]{:S(2)}) collective-permute-start(bf16[800,512]{1,0:T(8,128)(2,1)S(1)} %get-tuple-element.52), channel_id=1, source_target_pairs={{0,128},{128,0},{1,129},{129,1},{2,130},{130,2},{3,131},{131,3},{4... | collective-permute-start | bytes 2457608 | tf_op jit(solution)/shard_map/ppermute | solution.py:449
  10.6 3.8 %collective-permute-start.2 = (f32[1,128]{1,0:T(1,128)S(1)}, f32[1,128]{1,0:T(1,128)S(1)}, u32[]{:S(2)}, u32[]{:S(2)}) collective-permute-start(f32[1,128]{1,0:T(1,128)S(1)} %add_add_fusion._), channel_id=1, source_target_pairs={{0,3},{1,2},{2,1},{3,0},{4,7},{5,6},{6,5},{7,4},{8,11},{9,10},{10,... | collective-permute-start | bytes 1544 | tf_op jit(solution)/shard_map/ppermute | solution.py:428
